TPU v7x, 512 devices: a whole 4x8x8 slice. The times are simulated.
512 devices in a mesh: slab: 128 (over x_lo, z, y), chan: 4 (over x_hi, core).
Axes of the slice: x: 4 (x_hi: 2, x_lo: 2; x = x_hi * 2 + x_lo), y: 8, z: 8, core: 2. Of those that a mesh axis runs over, the one named last changes fastest.
Arguments:
- field_rows: bfloat16 [4, 512, 256, 512], P('chan', None, 'slab'), may hold values from -6 to 6
- region: int32 [128, 64], P('slab', 'chan'), may hold values 0 or 1
- first_kernel: bfloat16 [32, 4, 3, 3, 3], replicated, may hold values from -0.625 to 0.625
- first_bias: float32 [32], replicated, may hold values from -3 to 3
- second_kernel: bfloat16 [128, 32, 3, 3, 3], replicated, may hold values from -0.21875 to 0.21875
Outputs:
- latent: bfloat16 [128, 128, 64, 128], P('chan', 'slab')
All inputs are finite; a program needn't handle non-finite values. No bound on the sum of `region` on one device may be relied on, other than what follows from the above.
Results may differ from a plain program's by a relative error of at most 0.013.
Values may be sent and summed in bfloat16 or wider, within the bound.
No kernel may reach another device: no remote copies, remote signals or barrier semaphores. Data moves between devices by JAX's collectives and lax.ppermute only.
A program may use at most 128 MiB of HBM per device.

v0:
```python
import jax
import jax.numpy as jnp
from jax import lax
from jax.sharding import PartitionSpec as P


def shifted(block, axis, distance):
    devices = range(lax.axis_size(axis))
    route = [(i - distance, i) for i in devices if i - distance in devices]
    return lax.ppermute(block, axis, route)


def down_conv(source, kernel, padding, groups):
    return lax.conv_general_dilated(
        source[None],
        kernel,
        (2, 2, 2),
        padding,
        dimension_numbers=("NCDHW", "OIDHW", "NCDHW"),
        feature_group_count=groups,
        preferred_element_type=jnp.float32,
    )[0]


def body(field_rows, region, first_kernel, first_bias, second_kernel):
    slabs = lax.all_to_all(
        lax.all_to_all(field_rows, "slab", split_axis=1, concat_axis=2, tiled=True),
        "chan",
        split_axis=2,
        concat_axis=0,
        tiled=True,
    )
    cover = jnp.repeat(jnp.repeat(region, 4, 0), 4, 1).astype(jnp.bfloat16)
    slabs = slabs * cover[None, :, :, None]
    below = shifted(slabs[:, -1:], "slab", 1)
    widened = jnp.concatenate([below, slabs], 1)
    beside = shifted(widened[:, :, -1:], "chan", 1)
    widened = jnp.concatenate([beside, widened], 2)
    first = down_conv(widened, first_kernel, ((0, 0), (0, 0), (1, 0)), 1)
    hidden = jax.nn.silu(first + first_bias[:, None, None, None]).astype(jnp.bfloat16)
    groups = lax.axis_size("chan")
    width = second_kernel.shape[1] // groups
    mine = lax.all_to_all(hidden, "chan", split_axis=0, concat_axis=2, tiled=True)
    lower = shifted(mine[:, -1:], "slab", 1)
    mine = jnp.concatenate([lower, mine], 1)
    kernel_part = lax.dynamic_slice_in_dim(second_kernel, lax.axis_index("chan") * width, width, 1)
    return lax.psum_scatter(
        down_conv(mine, kernel_part, ((0, 0), (1, 0), (1, 0)), 1).astype(jnp.bfloat16),
        "chan",
        scatter_dimension=0,
        tiled=True,
    )


def solution(mesh):
    in_specs = (P("chan", None, "slab", None), P("slab", "chan"), P(), P(), P())
    out_specs = P("chan", "slab", None, None)
    return jax.shard_map(body, mesh=mesh, in_specs=in_specs, out_specs=out_specs, check_vma=False)
```

profile of v0, /device:TPU:1, one launch (start us, length us, event | category | flops | bytes accessed | tf_op | source)
XLA Modules:
  0.0 344.0 jit_solution(3507087665162403230)
XLA Ops:
  6.5 48.8 %all_to_all.54 = bf16[1,512,2,512]{3,2,0,1:T(2,128)(2,1)S(1)} all-to-all(bf16[1,512,2,512]{3,2,0,1:T(2,128)(2,1)} %bitcast.60), channel_id=1, replica_groups=mesh['slab'=128,'chan'=4] {'slab'}, dimensions={1} | all-to-all | bytes 2097152 | tf_op jit(solution)/shard_map/all_to_all | solution.py:27
  55.4 1.4 copy.35
  56.8 7.2 %all-to-all-start.1 = ((bf16[1,4,256,512]{3,1,0,2:T(4,128)(2,1)}), bf16[1,4,256,512]{3,1,0,2:T(4,128)(2,1)S(1)}, u32[]{:S(2)}, u32[]{:S(2)}) async-start(bf16[1,4,256,512]{3,1,0,2:T(4,128)(2,1)} %bitcast.4), calls=%async_computation.1 | async-start | bytes 2097152 | tf_op jit(solution)/shard_map/all_to_all | solution.py:26
  64.2 14.9 %all-to-all-done.1 = bf16[1,4,256,512]{3,1,0,2:T(4,128)(2,1)S(1)} async-done(((bf16[1,4,256,512]{3,1,0,2:T(4,128)(2,1)}), bf16[1,4,256,512]{3,1,0,2:T(4,128)(2,1)S(1)}, u32[]{:S(2)}, u32[]{:S(2)}) %all-to-all-start.1) | async-done | bytes 1048608 | tf_op jit(solution)/shard_map/all_to_all | solution.py:26
  80.6 3.2 collective-permute-start
  83.8 4.7 %collective-permute-done = bf16[4,1,64,512]{3,0,2,1:T(4,128)(2,1)S(1)} collective-permute-done((bf16[4,1,64,512]{3,0,2,1:T(4,128)(2,1)S(1)}, bf16[4,1,64,512]{3,0,2,1:T(4,128)(2,1)S(1)}, u32[]{:S(2)}, u32[]{:S(2)}) %collective-permute-start) | collective-permute-done | bytes 262176 | tf_op jit(solution)/shard_map/ppermute | solution.py:10
  88.5 3.9 %collective-permute-start.1 = (bf16[4,5,1,512]{3,0,2,1:T(4,128)(2,1)S(1)}, bf16[4,5,1,512]{3,0,2,1:T(4,128)(2,1)S(1)}, u32[]{:S(2)}, u32[]{:S(2)}) collective-permute-start(bf16[4,5,1,512]{3,0,2,1:T(4,128)(2,1)S(1)} %pad_maximum_fusion), channel_id=1, source_target_pairs={{0,1},{1,2},{2,3},{4,5},{5,6},{6,7},{8,9},{9,10},{10,11},{12,13},{... | collective-permute-start | bytes 61448 | tf_op jit(solution)/shard_map/ppermute | solution.py:10
  94.3 2.5 pad
  96.9 4.4 %reshape.23 = bf16[4,5,65,1,8,66]{5,4,0,2,1,3:T(8,128)(2,1)S(1)} reshape(bf16[4,5,65,1,528]{4,0,2,1,3:T(4,128)(2,1)} %pad) | data formatting | bytes 2745600 | tf_op jit(solution)/shard_map/conv_general_dilated | solution.py:14
  101.3 21.1 %copy.39 = bf16[4,5,65,1,8,66]{4,0,5,2,1,3:T(4,128)(2,1)} copy(bf16[4,5,65,1,8,66]{5,4,0,2,1,3:T(8,128)(2,1)S(1)} %reshape.23) | data formatting | bytes 2745600 | tf_op jit(solution)/shard_map/conv_general_dilated | solution.py:14
  122.4 1.5 slice.17
  124.0 65.7 %broadcast_select_fusion = f32[2,32,8,33,32]{4,2,3,1,0:T(8,128)} fusion(pred[8,33]{0,1:T(8,128)(4,1)S(1)} %copy-done.4, bf16[32,4,3,3,3]{0,1,4,3,2:T(4,128)(2,1)S(1)} %copy-done.2, bf16[4,5,65,1,7,2]{4,0,5,2,1,3:T(4,128)(2,1)S(1)} %slice.17, bf16[4,5,65,1,8,66]{4,0,5,2,1,3:T(4,128)(2,1)} %copy.39), kind=kOutput, calls=%fused_computation.13 | convolution fusion | flops 121569024 | bytes 3579064 | tf_op jit(solution)/shard_map/conv_general_dilated | solution.py:14
  189.7 9.8 %copy.40 = f32[2,32,8,33,32]{3,2,4,1,0:T(8,128)} copy(f32[2,32,8,33,32]{4,2,3,1,0:T(8,128)} %broadcast_select_fusion) | data formatting | bytes 4325376 | tf_op jit(solution)/shard_map/conv_general_dilated | solution.py:14
  199.5 6.1 %reshape.27 = f32[2,32,1,264,32]{3,4,1,0,2:T(8,128)S(1)} reshape(f32[2,32,8,33,32]{3,2,4,1,0:T(8,128)} %copy.40) | data formatting | bytes 4325376 | tf_op jit(solution)/shard_map/conv_general_dilated | solution.py:14
  206.9 20.3 %all_to_all.55 = bf16[32,2,32,256]{3,2,1,0:T(8,128)(2,1)S(1)} all-to-all(bf16[32,2,32,256]{3,2,1,0:T(8,128)(2,1)S(1)} %copy.41), channel_id=1, replica_groups=mesh['slab'=128,'chan'=4] {'chan'}, dimensions={0} | all-to-all | bytes 2097152 | tf_op jit(solution)/shard_map/all_to_all | solution.py:43
  227.3 4.0 %collective-permute-start.2 = (bf16[8,1,128,256]{3,2,1,0:T(8,128)(2,1)S(1)}, bf16[8,1,128,256]{3,2,1,0:T(8,128)(2,1)S(1)}, u32[]{:S(2)}, u32[]{:S(2)}) collective-permute-start(bf16[8,1,128,256]{3,2,1,0:T(8,128)(2,1)S(1)} %slice.19), channel_id=1, source_target_pairs={{0,4},{4,8},{8,12},{12,16},{16,20},{20,24},{24,28},{28,32},{32,36}... | collective-permute-start | bytes 1572872 | tf_op jit(solution)/shard_map/ppermute | solution.py:10
  231.4 10.1 %collective-permute-done.2 = bf16[8,1,128,256]{3,2,1,0:T(8,128)(2,1)S(1)} collective-permute-done((bf16[8,1,128,256]{3,2,1,0:T(8,128)(2,1)S(1)}, bf16[8,1,128,256]{3,2,1,0:T(8,128)(2,1)S(1)}, u32[]{:S(2)}, u32[]{:S(2)}) %collective-permute-start.2) | collective-permute-done | bytes 524320 | tf_op jit(solution)/shard_map/ppermute | solution.py:10
  241.6 1.9 copy.48
  243.6 1.5 pad.2.clone
  245.1 18.8 %copy.45 = bf16[8,3,128,1,8,34]{0,4,5,2,1,3:T(8,128)(2,1)} copy(bf16[8,3,128,1,8,34]{2,0,5,4,1,3:T(8,128)(2,1)S(1)} %bitcast.54) | data formatting | bytes 3342336 | tf_op jit(solution)/shard_map/conv_general_dilated | solution.py:14
  263.9 1.8 slice.20
  265.8 18.9 %select_convert_fusion = bf16[1,64,8,17,128]{4,2,3,1,0:T(8,128)(2,1)S(1)} fusion(pred[8,17]{0,1:T(8,128)(4,1)S(1)} %copy-done.5, bf16[8,3,128,1,7,2]{0,4,5,2,1,3:T(8,128)(2,1)S(1)} %slice.20, bf16[8,3,128,1,8,34]{0,4,5,2,1,3:T(8,128)(2,1)} %copy.45, bf16[128,32,3,3,3]{0,1,4,3,2:T(8,128)(2,1)S(1)} %copy-done, s32[]{:T(128)S(6)} %select_n.3), kind=kOutput, calls=%fused_computation.12 | convolution fusion | flops 486326272 | bytes 5530628 | tf_op jit(solution)/shard_map/conv_general_dilated | solution.py:14
  285.5 3.4 copy.47
  288.9 48.2 %reduce-scatter.2.cloned.1.call-done = bf16[32,1,64,128]{3,2,1,0:T(8,128)(2,1)} async-done(((bf16[128,1,64,128]{3,2,1,0:T(8,128)(2,1)}), bf16[32,1,64,128]{3,2,1,0:T(8,128)(2,1)}) %reduce-scatter.2.cloned.1.call-update) | async-done | bytes 524304 | tf_op jit(solution)/shard_map/reduce_scatter | solution.py:47
  (29 shorter events, 5.8 us)
Async XLA Ops:
  6.5 259.2 %copy-start = (bf16[128,32,3,3,3]{0,1,4,3,2:T(8,128)(2,1)S(1)}, bf16[128,32,3,3,3]{0,1,4,3,2:T(8,128)(2,1)}, u32[]{:S(2)}) copy-start(bf16[128,32,3,3,3]{0,1,4,3,2:T(8,128)(2,1)} %param.9) | copy-start | bytes 663556
  6.5 57.5 %copy-start.3 = (s32[1,16]{1,0:T(1,128)S(1)}, s32[1,16]{1,0:T(1,128)}, u32[]{:S(2)}) copy-start(s32[1,16]{1,0:T(1,128)} %param.6) | copy-start | bytes 196
  56.8 22.3 %all-to-all-start.1 = ((bf16[1,4,256,512]{3,1,0,2:T(4,128)(2,1)}), bf16[1,4,256,512]{3,1,0,2:T(4,128)(2,1)S(1)}, u32[]{:S(2)}, u32[]{:S(2)}) async-start(bf16[1,4,256,512]{3,1,0,2:T(4,128)(2,1)} %bitcast.4), calls=%async_computation.1 | async-start | bytes 2097152 | tf_op jit(solution)/shard_map/all_to_all | solution.py:26
  64.0 273.2 %reduce-scatter.2.cloned.1.call-start = ((), (), s32[]{:S(2)}) async-start(), calls=%async_computation.4 | async-start | bytes 2621440 | tf_op jit(solution)/shard_map/reduce_scatter | solution.py:47
  80.6 8.0 %collective-permute-start = (bf16[4,1,64,512]{3,0,2,1:T(4,128)(2,1)S(1)}, bf16[4,1,64,512]{3,0,2,1:T(4,128)(2,1)S(1)}, u32[]{:S(2)}, u32[]{:S(2)}) collective-permute-start(bf16[4,1,64,512]{3,0,2,1:T(4,128)(2,1)S(1)} %slice.16), channel_id=1, source_target_pairs={{0,4},{4,8},{8,12},{12,16},{16,20},{20,24},{24,28},{28,32},{32,36}... | collective-permute-start | bytes 786440 | tf_op jit(solution)/shard_map/ppermute | solution.py:10
  88.5 4.8 %collective-permute-start.1 = (bf16[4,5,1,512]{3,0,2,1:T(4,128)(2,1)S(1)}, bf16[4,5,1,512]{3,0,2,1:T(4,128)(2,1)S(1)}, u32[]{:S(2)}, u32[]{:S(2)}) collective-permute-start(bf16[4,5,1,512]{3,0,2,1:T(4,128)(2,1)S(1)} %pad_maximum_fusion), channel_id=1, source_target_pairs={{0,1},{1,2},{2,3},{4,5},{5,6},{6,7},{8,9},{9,10},{10,11},{12,13},{... | collective-permute-start | bytes 61448 | tf_op jit(solution)/shard_map/ppermute | solution.py:10
  101.3 22.7 %copy-start.2 = (bf16[32,4,3,3,3]{0,1,4,3,2:T(4,128)(2,1)S(1)}, bf16[32,4,3,3,3]{0,1,4,3,2:T(4,128)(2,1)}, u32[]{:S(2)}) copy-start(bf16[32,4,3,3,3]{0,1,4,3,2:T(4,128)(2,1)} %param.7) | copy-start | bytes 20740
  101.3 22.7 %copy-start.4 = (pred[8,33]{0,1:T(8,128)(4,1)S(1)}, pred[8,33]{0,1:T(8,128)(4,1)}, u32[]{:S(2)}) copy-start(pred[8,33]{0,1:T(8,128)(4,1)} %constant.24) | copy-start | bytes 796
  199.5 6.1 %copy-start.1 = (f32[32]{0:T(128)S(1)}, f32[32]{0:T(128)}, u32[]{:S(2)}) copy-start(f32[32]{0:T(128)} %param.8) | copy-start | bytes 388
  227.3 14.2 %collective-permute-start.2 = (bf16[8,1,128,256]{3,2,1,0:T(8,128)(2,1)S(1)}, bf16[8,1,128,256]{3,2,1,0:T(8,128)(2,1)S(1)}, u32[]{:S(2)}, u32[]{:S(2)}) collective-permute-start(bf16[8,1,128,256]{3,2,1,0:T(8,128)(2,1)S(1)} %slice.19), channel_id=1, source_target_pairs={{0,4},{4,8},{8,12},{12,16},{16,20},{20,24},{24,28},{28,32},{32,36}... | collective-permute-start | bytes 1572872 | tf_op jit(solution)/shard_map/ppermute | solution.py:10
  245.1 20.7 %copy-start.5 = (pred[8,17]{0,1:T(8,128)(4,1)S(1)}, pred[8,17]{0,1:T(8,128)(4,1)}, u32[]{:S(2)}) copy-start(pred[8,17]{0,1:T(8,128)(4,1)} %constant.23) | copy-start | bytes 412
Sparse Core Ops, SparseCore 0:
  289.0 48.0 reduce-scatter.1
where the time goes:
time: 345 us; the launch traced here: 344 us
  matrix products  84.6 us (25%)
  waiting for transfers between devices  78.9 us (23%)
  local copies, waits for them, and re-layouts  76.2 us (22%)
  blocking collectives  69.1 us (20%)
  starting transfers between devices  18.4 us (5%)
  between operations  13.6 us (4%)
    conv_general_dilated x2, matrix products, down_conv(): lax.conv_general_dilated(source[None], kernel, (2, 2, 2), padding, dimens...  84.6 us
    conv_general_dilated x7, local copies, waits for them, and re-layouts, down_conv(): lax.conv_general_dilated(source[None], kernel, (2, 2, 2), padding, dimens...  63.7 us
    all_to_all x1, blocking collectives, body(): lax.all_to_all(field_rows, 'slab', split_axis=1, concat_axis=2, tiled=True)  48.8 us
    reduce_scatter x1, waiting for transfers between devices, body(): lax.psum_scatter(down_conv(mine, kernel_part, ((0, 0), (1, 0), (1, 0)), 1...  48.2 us
    all_to_all x1, blocking collectives, body(): lax.all_to_all(hidden, 'chan', split_axis=0, concat_axis=2, tiled=True)  20.3 us
    ppermute x3, waiting for transfers between devices, shifted(): return lax.ppermute(block, axis, route)  15.7 us
    all_to_all x1, waiting for transfers between devices, body(): lax.all_to_all(lax.all_to_all(field_rows, 'slab', split_axis=1, concat_ax...  14.9 us
    ppermute x3, starting transfers between devices, shifted(): return lax.ppermute(block, axis, route)  11.2 us
  transfers between devices with their start and end apart: 5, of which 5 were waited for; matrix products, arithmetic and copies ran while one was open for 0% of the time, Pallas kernels for 0%

commit v1 on v0

v1 whole, which is shorter than its diff:
```python
import functools

import jax
import jax.numpy as jnp
import numpy as np
from jax import lax
from jax.experimental import pallas as pl
from jax.experimental.pallas import tpu as pltpu
from jax.sharding import Mesh, PartitionSpec as P

FINE = ("x_lo", "z_hi", "z_lo", "y", "x_hi", "core")
SHAPE = (2, 2, 4, 8, 2, 2)
REGION = ("z_lo", "y", "x_hi", "core")
BF = jnp.bfloat16
F32 = jnp.float32


def encoder(block, slab):
    x_lo, z_hi, z_lo, y = slab >> 6, (slab >> 5) & 1, (slab >> 3) & 3, slab & 7
    return (((block * 4 + z_lo) * 8 + y) * 2 + x_lo) * 2 + z_hi


PAIRS = [(b, s) for b in range(4) for s in range(128)]
REGION_ROUTE = [(s * 4 + b, encoder(b, s)) for b, s in PAIRS]
Z_ROUTE = [(encoder(b, s), encoder(b, s + 1)) for b, s in PAIRS if s < 127]
Y_ROUTE = [(encoder(b, s), encoder(b + 1, s)) for b, s in PAIRS if b < 3]
ZY_ROUTE = [(encoder(b, s), encoder(b + 1, s + 1)) for b, s in PAIRS if b < 3 and s < 127]
OUT_ROUTES = [[(encoder(b, s), s * 4 + (b ^ i)) for b, s in PAIRS] for i in range(4)]


def one_hots():
    phases = np.zeros((512, 512), np.float32)
    for x in range(512):
        phases[x, (x % 4) * 128 + x // 4] = 1
    shift = np.zeros((128, 128), np.float32)
    for q in range(127):
        shift[q, q + 1] = 1
    upper = np.zeros((48, 64), np.float32)
    for group in range(8):
        for row in range(6):
            upper[group * 6 + row, group * 8 + 2 + row] = 1
    own = np.zeros((2, 2, 2, 3, 3, 3, 4, 5, 3, 4, 4, 2), np.float32)
    halo = np.zeros((2, 2, 2, 3, 3, 3, 4, 5, 4, 4, 3, 2), np.float32)
    for n in range(2):
        for par in range(2):
            for ky in range(3):
                t, yy = (n, 1) if ky == 0 else (n + 1, ky - 1)
                for kx in range(3):
                    r = 2 * par + kx
                    for c in range(4):
                        for plane, kz, z in ((0, 1, 0), (0, 2, 1), (1, 0, 1), (1, 1, 2), (1, 2, 3)):
                            own[plane, n, par, kz, ky, kx, c, r, t, c, z, yy] = 1
                        for plane, kz, z in ((0, 0, 1), (0, 1, 2), (0, 2, 3), (1, 0, 3)):
                            halo[plane, n, par, kz, ky, kx, c, r, t, c, z - 1, yy] = 1
    return phases, shift, upper, own.reshape(8, 108, 480), halo.reshape(8, 108, 480)


def dot(a, b):
    return jnp.dot(a, b, preferred_element_type=F32)


def split_phases(field_ref, phases_ref, out_ref):
    rows = field_ref[...]
    out_ref[...] = dot(rows, phases_ref[...]).astype(BF).reshape(32, 1, 8, 512)


def mask_rows(region_ref, rows_ref, upper_ref, masked_ref, halo_ref):
    for pair in range(16):
        keep = region_ref[0, pair].astype(F32).astype(BF)
        rows = rows_ref[64 * pair : 64 * pair + 64, :] * keep
        masked_ref[64 * pair : 64 * pair + 64, :] = rows
        halo_ref[48 * pair : 48 * pair + 48, :] = dot(upper_ref[...], rows).astype(BF)


def encode(place_ref, own_ref, zed_ref, why_ref, both_ref, own_kernel_ref, halo_kernel_ref, bias_ref, second_ref, shift_ref, out_ref, own_first, zed_first, hidden, latent):
    block, slab = place_ref[0], place_ref[1]
    shift = shift_ref[...]
    own_first[0:64, :] = dot(why_ref[:, 384:512], shift).astype(BF)
    own_first[64:1088, :] = dot(own_ref[:, 384:512], shift).astype(BF)
    zed_first[0:48, :] = dot(both_ref[:, 384:512], shift).astype(BF)
    zed_first[48:816, :] = dot(zed_ref[:, 384:512], shift).astype(BF)
    bias = bias_ref[...]
    low_plane = jnp.where(slab == 0, 0.0, 1.0).astype(F32)
    low_row = jnp.where(block == 0, 0.0, 1.0).astype(F32)

    def silu(v):
        half = 0.5 * (v + bias)
        return half + half * jnp.tanh(half)

    def operand(first, edge_ref, rows_ref, edge, start, stop):
        pieces = [first[start:stop, :]]
        for r in range(4):
            lanes = slice(128 * r, 128 * r + 128)
            if start < edge:
                pieces += [edge_ref[start:edge, lanes], rows_ref[0 : stop - edge, lanes]]
            else:
                pieces.append(rows_ref[start - edge : stop - edge, lanes])
        return jnp.concatenate(pieces, 0)

    for p in range(17):
        if p < 16:
            own = operand(own_first, why_ref, own_ref, 64, 64 * p, 64 * p + 96)
            zed = operand(zed_first, both_ref, zed_ref, 48, 48 * p, 48 * p + 96)
            upper = dot(own_kernel_ref[...], own)
            lower = dot(halo_kernel_ref[...], zed)
            planes = (lower[0:128], upper[0:128] + lower[128:256], upper[128:256])
        else:
            own = operand(own_first, why_ref, own_ref, 64, 1024, 1088)
            zed = operand(zed_first, both_ref, zed_ref, 48, 768, 816)
            own_w = jnp.concatenate([own_kernel_ref[:, 96 * r : 96 * r + 64] for r in range(5)], 1)
            zed_w = jnp.concatenate([halo_kernel_ref[:, 96 * r : 96 * r + 48] for r in range(5)], 1)
            upper = dot(own_w, own)
            lower = dot(zed_w, zed)
            planes = (lower[0:64], upper[0:64] + lower[128:192], upper[128:192])
        for kz, plane in enumerate(planes):
            rows = plane.shape[0]
            half = 0.5 * (plane + bias[0:rows])
            value = half + half * jnp.tanh(half)
            if kz == 0:
                value = value * low_plane
            if p == 0:
                value = jnp.concatenate([value[0:64] * low_row, value[64:128]], 0)
            hidden[kz, 128 * p : 128 * p + rows, :] = value.astype(BF)

    lane = lax.broadcasted_iota(jnp.int32, (128, 128), 1)
    for o in range(16):
        taps = jnp.concatenate([hidden[kz, 128 * o : 128 * o + 192, :] for kz in range(3)], 0)
        both = dot(second_ref[...], taps)
        earlier = jnp.where(lane == 0, 0.0, pltpu.roll(both[128:256], 1, 1))
        latent[:, o, :] = both[0:128] + earlier
    for g in range(4):
        out_ref[block ^ g] = latent[32 * g : 32 * g + 32].astype(BF)


def join_blocks(place_ref, a_ref, b_ref, c_ref, d_ref, out_ref):
    group = place_ref[0]
    for i, ref in enumerate((a_ref, b_ref, c_ref, d_ref)):
        start = pl.multiple_of((group ^ i) * 16, 16)
        out_ref[:, pl.ds(start, 16), :] = ref[...]


VMEM = pl.BlockSpec(memory_space=pltpu.VMEM)
SMEM = pl.BlockSpec(memory_space=pltpu.SMEM)
PARAMS = pltpu.CompilerParams(vmem_limit_bytes=32 * 1024 * 1024)


def body(field_rows, region, first_kernel, first_bias, second_kernel):
    phases, shift, upper, own_hot, halo_hot = (jnp.asarray(a, BF) for a in one_hots())
    block = lax.axis_index("x_lo") * 2 + lax.axis_index("z_hi")
    inner = lax.axis_index("x_hi") * 2 + lax.axis_index("core")
    slab = inner * 32 + lax.axis_index("z_lo") * 8 + lax.axis_index("y")
    place = jnp.stack([block, slab]).astype(jnp.int32)

    keep = lax.ppermute(region, FINE, REGION_ROUTE)
    split = pl.pallas_call(
        split_phases,
        grid=(4,),
        in_specs=[pl.BlockSpec((256, 512), lambda i: (i, 0)), pl.BlockSpec((512, 512), lambda i: (0, 0))],
        out_specs=pl.BlockSpec((32, 1, 8, 512), lambda i: (0, i, 0, 0)),
        out_shape=jax.ShapeDtypeStruct((32, 4, 8, 512), BF),
        compiler_params=PARAMS,
    )(field_rows.reshape(1024, 512), phases)
    rows = lax.all_to_all(split.reshape(128, 8, 512), REGION, split_axis=0, concat_axis=0, tiled=True)
    own, upper_rows = pl.pallas_call(
        mask_rows,
        in_specs=[SMEM, VMEM, VMEM],
        out_specs=[VMEM, VMEM],
        out_shape=[jax.ShapeDtypeStruct((1024, 512), BF), jax.ShapeDtypeStruct((768, 512), BF)],
        compiler_params=PARAMS,
    )(keep, rows.reshape(1024, 512), upper)
    zed = lax.ppermute(upper_rows, FINE, Z_ROUTE)
    why = lax.ppermute(own[960:1024], FINE, Y_ROUTE)
    both = lax.ppermute(upper_rows[720:768], FINE, ZY_ROUTE)

    taps = first_kernel.transpose(2, 3, 4, 1, 0).reshape(108, 32)
    own_kernel = jnp.einsum("kh,bkm->bhm", taps, own_hot, preferred_element_type=F32).astype(BF).reshape(256, 480)
    halo_kernel = jnp.einsum("kh,bkm->bhm", taps, halo_hot, preferred_element_type=F32).astype(BF).reshape(256, 480)
    bias = jnp.broadcast_to(jnp.tile(first_bias, 4)[:, None], (128, 128))
    second = second_kernel.transpose(0, 2, 3, 4, 1).reshape(128, 9, 3, 32)
    straight = second[:, :, 1:3].reshape(128, 576)
    earlier = jnp.pad(second[:, :, 0:1], ((0, 0), (0, 0), (1, 0), (0, 0))).reshape(128, 576)
    second = jnp.concatenate([straight, earlier], 0)

    pieces = pl.pallas_call(
        encode,
        in_specs=[SMEM] + [VMEM] * 9,
        out_specs=VMEM,
        out_shape=jax.ShapeDtypeStruct((4, 32, 16, 128), BF),
        scratch_shapes=[
            pltpu.VMEM((1088, 128), BF),
            pltpu.VMEM((816, 128), BF),
            pltpu.VMEM((3, 2112, 128), BF),
            pltpu.VMEM((128, 16, 128), F32),
        ],
        compiler_params=PARAMS,
    )(place, own, zed, why, both, own_kernel, halo_kernel, bias, second, shift)
    moved = [lax.ppermute(pieces[i], FINE, OUT_ROUTES[i]) for i in range(4)]
    joined = pl.pallas_call(
        join_blocks,
        in_specs=[SMEM] + [VMEM] * 4,
        out_specs=VMEM,
        out_shape=jax.ShapeDtypeStruct((32, 64, 128), BF),
        compiler_params=PARAMS,
    )(inner.astype(jnp.int32).reshape(1), *moved)
    return joined.reshape(32, 1, 64, 128)


def solution(mesh):
    fine = Mesh(mesh.devices.reshape(SHAPE), FINE)
    slab, chan = FINE[:4], FINE[4:]
    in_specs = (P(chan, None, slab, None), P(slab, chan), P(), P(), P())
    out_specs = P(chan, slab, None, None)
    return jax.shard_map(body, mesh=fine, in_specs=in_specs, out_specs=out_specs, check_vma=False)
```

time: 345 us -> 118 us (0.34)
  the two profiles are of different devices: /device:TPU:1 before, /device:TPU:2 now
where the time goes in v1:
time: 118 us; the launch traced here: 117 us
  waiting for transfers between devices  51 us (43%)
  starting transfers between devices  49.5 us (42%)
  Pallas kernels  9.89 us (8%)
  local copies, waits for them, and re-layouts  5.67 us (5%)
    all_to_all x1, waiting for transfers between devices, body(): lax.all_to_all(split.reshape(128, 8, 512), REGION, split_axis=0, concat_a...  25.2 us
    all_to_all x1, starting transfers between devices, body(): lax.all_to_all(split.reshape(128, 8, 512), REGION, split_axis=0, concat_a...  16.4 us
    ppermute x4, starting transfers between devices, body(): moved = [lax.ppermute(pieces[i], FINE, OUT_ROUTES[i]) for i in range(4)]  16.3 us
    ppermute x1, waiting for transfers between devices, body(): why = lax.ppermute(own[960:1024], FINE, Y_ROUTE)  10.4 us
    ppermute x4, waiting for transfers between devices, body(): moved = [lax.ppermute(pieces[i], FINE, OUT_ROUTES[i]) for i in range(4)]  9.76 us
    ppermute x1, starting transfers between devices, body(): why = lax.ppermute(own[960:1024], FINE, Y_ROUTE)  8.23 us
    pallas_call x1, Pallas kernels, body(): pl.pallas_call(encode, in_specs=[SMEM] + [VMEM] * 9, out_specs=VMEM, out_...  4.81 us
    ppermute x1, waiting for transfers between devices, body(): both = lax.ppermute(upper_rows[720:768], FINE, ZY_ROUTE)  4.18 us
  transfers between devices with their start and end apart: 9, of which 5 were waited for; matrix products, arithmetic and copies ran while one was open for 2% of the time, Pallas kernels for 0%

profile of v1, /device:TPU:2, one launch (start us, length us, event | category | flops | bytes accessed | tf_op | source)
XLA Modules:
  0.0 117.1 jit_solution(8249063738761099530)
XLA Ops:
  0.0 1.5 %reshape.36.field_ref = bf16[1024,512]{1,0:T(8,128)(2,1)S(1)} reshape(bf16[1,512,2,512]{3,2,1,0:T(2,128)(2,1)} %param.10) | data formatting | bytes 2097152 | tf_op jit(solution)/shard_map/reshape | solution.py:162
  1.5 2.4 %shard_map.100 = bf16[32,4,8,512]{3,2,1,0:T(8,128)(2,1)} custom-call(bf16[1024,512]{1,0:T(8,128)(2,1)S(1)} %reshape.36.field_ref, bf16[512,512]{1,0:T(8,128)(2,1)S(1)} %copy-done), custom_call_target="tpu_custom_call" | custom-call | tf_op jit(solution)/shard_map/pallas_call | solution.py:155
  4.0 16.4 %all-to-all-start = ((bf16[128,8,512]{2,1,0:T(8,128)(2,1)}), bf16[128,8,512]{2,1,0:T(8,128)(2,1)S(1)}, u32[]{:S(2)}, u32[]{:S(2)}) async-start(bf16[128,8,512]{2,1,0:T(8,128)(2,1)} %bitcast.3), calls=%async_computation | async-start | bytes 2097152 | tf_op jit(solution)/shard_map/all_to_all | solution.py:163
  20.4 3.9 %collective-permute-start = (s32[1,16]{1,0:T(1,128)S(1)}, s32[1,16]{1,0:T(1,128)S(1)}, u32[]{:S(2)}, u32[]{:S(2)}) collective-permute-start(s32[1,16]{1,0:T(1,128)S(1)} %copy-done.8), channel_id=1, source_target_pairs={{0,0},{4,4},{8,8},{12,12},{16,16},{20,20},{24,24},{28,28},{32,32},... | collective-permute-start | bytes 200 | tf_op jit(solution)/shard_map/ppermute | solution.py:154
  24.3 1.5 %collective-permute-done.region_ref = s32[1,16]{1,0:T(1,128)S(1)} collective-permute-done((s32[1,16]{1,0:T(1,128)S(1)}, s32[1,16]{1,0:T(1,128)S(1)}, u32[]{:S(2)}, u32[]{:S(2)}) %collective-permute-start) | collective-permute-done | bytes 96 | tf_op jit(solution)/shard_map/ppermute | solution.py:154
  25.9 25.2 %all-to-all-done = bf16[128,8,512]{2,1,0:T(8,128)(2,1)S(1)} async-done(((bf16[128,8,512]{2,1,0:T(8,128)(2,1)}), bf16[128,8,512]{2,1,0:T(8,128)(2,1)S(1)}, u32[]{:S(2)}, u32[]{:S(2)}) %all-to-all-start) | async-done | bytes 1048608 | tf_op jit(solution)/shard_map/all_to_all | solution.py:163
  51.0 1.8 %shard_map.101 = (bf16[1024,512]{1,0:T(8,128)(2,1)S(1)}, bf16[768,512]{1,0:T(8,128)(2,1)}) custom-call(s32[1,16]{1,0:T(1,128)S(1)} %collective-permute-done.region_ref, bf16[1024,512]{1,0:T(8,128)(2,1)S(1)} %bitcast.36, bf16[48,64]{1,0:T(8,128)(2,1)S(1)} %copy-done.2), custom_call_target="tpu_custom_call" | custom-call | tf_op jit(solution)/shard_map/pallas_call | solution.py:164
  52.8 2.9 %collective-permute-start.1 = (bf16[768,512]{1,0:T(8,128)(2,1)}, bf16[768,512]{1,0:T(8,128)(2,1)S(1)}, u32[]{:S(2)}, u32[]{:S(2)}) collective-permute-start(bf16[768,512]{1,0:T(8,128)(2,1)} %get-tuple-element.8), channel_id=1, source_target_pairs={{0,4},{4,8},{8,12},{12,16},{16,20},{20,24},{24,28},{28,32},{32,36}... | collective-permute-start | bytes 2359304 | tf_op jit(solution)/shard_map/ppermute | solution.py:171
  56.2 0.6 copy-done.6
  57.3 0.8 copy-done.3
  58.4 0.8 slice.25
  59.2 8.2 %collective-permute-start.2 = (bf16[64,512]{1,0:T(8,128)(2,1)S(1)}, bf16[64,512]{1,0:T(8,128)(2,1)S(1)}, u32[]{:S(2)}, u32[]{:S(2)}) collective-permute-start(bf16[64,512]{1,0:T(8,128)(2,1)S(1)} %slice.24), channel_id=1, source_target_pairs={{0,128},{4,132},{8,136},{12,140},{16,144},{20,148},{24,152},{28,15... | collective-permute-start | bytes 196616 | tf_op jit(solution)/shard_map/ppermute | solution.py:172
  67.4 1.8 %collective-permute-start.3 = (bf16[48,512]{1,0:T(8,128)(2,1)S(1)}, bf16[48,512]{1,0:T(8,128)(2,1)S(1)}, u32[]{:S(2)}, u32[]{:S(2)}) collective-permute-start(bf16[48,512]{1,0:T(8,128)(2,1)S(1)} %slice.25), channel_id=1, source_target_pairs={{0,132},{4,136},{8,140},{12,144},{16,148},{20,152},{24,156},{28,16... | collective-permute-start | bytes 147464 | tf_op jit(solution)/shard_map/ppermute | solution.py:173
  69.3 0.6 copy-done.7
  70.0 4.2 %collective-permute-done.3.both_ref = bf16[48,512]{1,0:T(8,128)(2,1)S(1)} collective-permute-done((bf16[48,512]{1,0:T(8,128)(2,1)S(1)}, bf16[48,512]{1,0:T(8,128)(2,1)S(1)}, u32[]{:S(2)}, u32[]{:S(2)}) %collective-permute-start.3) | collective-permute-done | bytes 49184 | tf_op jit(solution)/shard_map/ppermute | solution.py:173
  74.1 10.4 %collective-permute-done.2.why_ref = bf16[64,512]{1,0:T(8,128)(2,1)S(1)} collective-permute-done((bf16[64,512]{1,0:T(8,128)(2,1)S(1)}, bf16[64,512]{1,0:T(8,128)(2,1)S(1)}, u32[]{:S(2)}, u32[]{:S(2)}) %collective-permute-start.2) | collective-permute-done | bytes 65568 | tf_op jit(solution)/shard_map/ppermute | solution.py:172
  84.6 0.7 copy-done.1
  85.3 4.8 %shard_map.102 = bf16[4,32,16,128]{3,2,1,0:T(8,128)(2,1)S(1)} custom-call(s32[2]{0:T(128)S(1)} %pad_add_fusion.place_ref, bf16[1024,512]{1,0:T(8,128)(2,1)S(1)} %get-tuple-element.7.own_ref, bf16[768,512]{1,0:T(8,128)(2,1)S(1)} %collective-permute-done.1.zed_ref, bf16[64,512]{1,0:T(8,128)(2,1)S(1)} %collective-permute-done.2.why_ref, ...), custom_call_target="tpu_custom_call" | custom-call | tf_op jit(solution)/shard_map/pallas_call | solution.py:184
  90.1 1.9 %collective-permute-start.4 = (bf16[32,16,128]{2,1,0:T(8,128)(2,1)S(1)}, bf16[32,16,128]{2,1,0:T(8,128)(2,1)S(1)}, u32[]{:S(2)}, u32[]{:S(2)}) collective-permute-start(bf16[32,16,128]{2,1,0:T(8,128)(2,1)S(1)} %get-tuple-element.12), channel_id=1, source_target_pairs={{0,0},{4,4},{8,8},{12,12},{16,16},{20,20},{24,24},{28,28},{32,32},... | collective-permute-start | bytes 393224 | tf_op jit(solution)/shard_map/ppermute | solution.py:197
  92.0 1.9 %collective-permute-start.5 = (bf16[32,16,128]{2,1,0:T(8,128)(2,1)S(1)}, bf16[32,16,128]{2,1,0:T(8,128)(2,1)S(1)}, u32[]{:S(2)}, u32[]{:S(2)}) collective-permute-start(bf16[32,16,128]{2,1,0:T(8,128)(2,1)S(1)} %get-tuple-element.11), channel_id=1, source_target_pairs={{0,1},{4,5},{8,9},{12,13},{16,17},{20,21},{24,25},{28,29},{32,33},... | collective-permute-start | bytes 393224 | tf_op jit(solution)/shard_map/ppermute | solution.py:197
  94.0 2.1 %collective-permute-start.6 = (bf16[32,16,128]{2,1,0:T(8,128)(2,1)S(1)}, bf16[32,16,128]{2,1,0:T(8,128)(2,1)S(1)}, u32[]{:S(2)}, u32[]{:S(2)}) collective-permute-start(bf16[32,16,128]{2,1,0:T(8,128)(2,1)S(1)} %get-tuple-element.10), channel_id=1, source_target_pairs={{0,2},{4,6},{8,10},{12,14},{16,18},{20,22},{24,26},{28,30},{32,34}... | collective-permute-start | bytes 393224 | tf_op jit(solution)/shard_map/ppermute | solution.py:197
  96.1 10.4 %collective-permute-start.7 = (bf16[32,16,128]{2,1,0:T(8,128)(2,1)S(1)}, bf16[32,16,128]{2,1,0:T(8,128)(2,1)S(1)}, u32[]{:S(2)}, u32[]{:S(2)}) collective-permute-start(bf16[32,16,128]{2,1,0:T(8,128)(2,1)S(1)} %get-tuple-element.9), channel_id=1, source_target_pairs={{0,3},{4,7},{8,11},{12,15},{16,19},{20,23},{24,27},{28,31},{32,35}... | collective-permute-start | bytes 393224 | tf_op jit(solution)/shard_map/ppermute | solution.py:197
  106.4 9.8 %collective-permute-done.7.d_ref = bf16[32,16,128]{2,1,0:T(8,128)(2,1)S(1)} collective-permute-done((bf16[32,16,128]{2,1,0:T(8,128)(2,1)S(1)}, bf16[32,16,128]{2,1,0:T(8,128)(2,1)S(1)}, u32[]{:S(2)}, u32[]{:S(2)}) %collective-permute-start.7) | collective-permute-done | bytes 131104 | tf_op jit(solution)/shard_map/ppermute | solution.py:197
  116.2 0.9 shard_map.103
  (33 shorter events, 1.4 us)
Async XLA Ops:
  0.0 1.5 %copy-start = (bf16[512,512]{1,0:T(8,128)(2,1)S(1)}, bf16[512,512]{1,0:T(8,128)(2,1)}, u32[]{:S(2)}) copy-start(bf16[512,512]{1,0:T(8,128)(2,1)} %constant.43.clone.phases_ref) | copy-start | bytes 1572868
  4.0 16.5 %copy-start.8 = (s32[1,16]{1,0:T(1,128)S(1)}, s32[1,16]{1,0:T(1,128)}, u32[]{:S(2)}) copy-start(s32[1,16]{1,0:T(1,128)} %param.11) | copy-start | bytes 196
  4.0 47.1 %copy-start.2 = (bf16[48,64]{1,0:T(8,128)(2,1)S(1)}, bf16[48,64]{1,0:T(8,128)(2,1)}, u32[]{:S(2)}) copy-start(bf16[48,64]{1,0:T(8,128)(2,1)} %constant.45.clone.upper_ref) | copy-start | bytes 18436
  4.0 47.1 %all-to-all-start = ((bf16[128,8,512]{2,1,0:T(8,128)(2,1)}), bf16[128,8,512]{2,1,0:T(8,128)(2,1)S(1)}, u32[]{:S(2)}, u32[]{:S(2)}) async-start(bf16[128,8,512]{2,1,0:T(8,128)(2,1)} %bitcast.3), calls=%async_computation | async-start | bytes 2097152 | tf_op jit(solution)/shard_map/all_to_all | solution.py:163
  20.4 5.4 %collective-permute-start = (s32[1,16]{1,0:T(1,128)S(1)}, s32[1,16]{1,0:T(1,128)S(1)}, u32[]{:S(2)}, u32[]{:S(2)}) collective-permute-start(s32[1,16]{1,0:T(1,128)S(1)} %copy-done.8), channel_id=1, source_target_pairs={{0,0},{4,4},{8,8},{12,12},{16,16},{20,20},{24,24},{28,28},{32,32},... | collective-permute-start | bytes 200 | tf_op jit(solution)/shard_map/ppermute | solution.py:154
  51.0 4.7 %copy-start.5 = (bf16[128,32,3,3,3]{0,1,4,3,2:T(8,128)(2,1)S(1)}, bf16[128,32,3,3,3]{0,1,4,3,2:T(8,128)(2,1)}, u32[]{:S(2)}) copy-start(bf16[128,32,3,3,3]{0,1,4,3,2:T(8,128)(2,1)} %param.14) | copy-start | bytes 663556
  52.8 31.7 %collective-permute-start.1 = (bf16[768,512]{1,0:T(8,128)(2,1)}, bf16[768,512]{1,0:T(8,128)(2,1)S(1)}, u32[]{:S(2)}, u32[]{:S(2)}) collective-permute-start(bf16[768,512]{1,0:T(8,128)(2,1)} %get-tuple-element.8), channel_id=1, source_target_pairs={{0,4},{4,8},{8,12},{12,16},{16,20},{20,24},{24,28},{28,32},{32,36}... | collective-permute-start | bytes 2359304 | tf_op jit(solution)/shard_map/ppermute | solution.py:171
  55.8 1.2 %copy-start.4 = (bf16[8,108,480]{2,1,0:T(8,128)(2,1)S(1)}, bf16[8,108,480]{2,1,0:T(8,128)(2,1)}, u32[]{:S(2)}) copy-start(bf16[8,108,480]{2,1,0:T(8,128)(2,1)} %constant.47.clone) | copy-start | bytes 2488324
  56.0 0.8 copy-start.6
  56.8 1.2 %copy-start.3 = (bf16[8,108,480]{2,1,0:T(8,128)(2,1)S(1)}, bf16[8,108,480]{2,1,0:T(8,128)(2,1)}, u32[]{:S(2)}) copy-start(bf16[8,108,480]{2,1,0:T(8,128)(2,1)} %constant.46.clone) | copy-start | bytes 2488324
  59.2 25.3 %collective-permute-start.2 = (bf16[64,512]{1,0:T(8,128)(2,1)S(1)}, bf16[64,512]{1,0:T(8,128)(2,1)S(1)}, u32[]{:S(2)}, u32[]{:S(2)}) collective-permute-start(bf16[64,512]{1,0:T(8,128)(2,1)S(1)} %slice.24), channel_id=1, source_target_pairs={{0,128},{4,132},{8,136},{12,140},{16,144},{20,148},{24,152},{28,15... | collective-permute-start | bytes 196616 | tf_op jit(solution)/shard_map/ppermute | solution.py:172
  67.4 6.7 %collective-permute-start.3 = (bf16[48,512]{1,0:T(8,128)(2,1)S(1)}, bf16[48,512]{1,0:T(8,128)(2,1)S(1)}, u32[]{:S(2)}, u32[]{:S(2)}) collective-permute-start(bf16[48,512]{1,0:T(8,128)(2,1)S(1)} %slice.25), channel_id=1, source_target_pairs={{0,132},{4,136},{8,140},{12,144},{16,148},{20,152},{24,156},{28,16... | collective-permute-start | bytes 147464 | tf_op jit(solution)/shard_map/ppermute | solution.py:173
  69.2 0.7 copy-start.7
  84.5 0.8 copy-start.1
  90.1 16.3 %collective-permute-start.4 = (bf16[32,16,128]{2,1,0:T(8,128)(2,1)S(1)}, bf16[32,16,128]{2,1,0:T(8,128)(2,1)S(1)}, u32[]{:S(2)}, u32[]{:S(2)}) collective-permute-start(bf16[32,16,128]{2,1,0:T(8,128)(2,1)S(1)} %get-tuple-element.12), channel_id=1, source_target_pairs={{0,0},{4,4},{8,8},{12,12},{16,16},{20,20},{24,24},{28,28},{32,32},... | collective-permute-start | bytes 393224 | tf_op jit(solution)/shard_map/ppermute | solution.py:197
  92.0 14.4 %collective-permute-start.5 = (bf16[32,16,128]{2,1,0:T(8,128)(2,1)S(1)}, bf16[32,16,128]{2,1,0:T(8,128)(2,1)S(1)}, u32[]{:S(2)}, u32[]{:S(2)}) collective-permute-start(bf16[32,16,128]{2,1,0:T(8,128)(2,1)S(1)} %get-tuple-element.11), channel_id=1, source_target_pairs={{0,1},{4,5},{8,9},{12,13},{16,17},{20,21},{24,25},{28,29},{32,33},... | collective-permute-start | bytes 393224 | tf_op jit(solution)/shard_map/ppermute | solution.py:197
  94.0 12.5 %collective-permute-start.6 = (bf16[32,16,128]{2,1,0:T(8,128)(2,1)S(1)}, bf16[32,16,128]{2,1,0:T(8,128)(2,1)S(1)}, u32[]{:S(2)}, u32[]{:S(2)}) collective-permute-start(bf16[32,16,128]{2,1,0:T(8,128)(2,1)S(1)} %get-tuple-element.10), channel_id=1, source_target_pairs={{0,2},{4,6},{8,10},{12,14},{16,18},{20,22},{24,26},{28,30},{32,34}... | collective-permute-start | bytes 393224 | tf_op jit(solution)/shard_map/ppermute | solution.py:197
  96.1 20.1 %collective-permute-start.7 = (bf16[32,16,128]{2,1,0:T(8,128)(2,1)S(1)}, bf16[32,16,128]{2,1,0:T(8,128)(2,1)S(1)}, u32[]{:S(2)}, u32[]{:S(2)}) collective-permute-start(bf16[32,16,128]{2,1,0:T(8,128)(2,1)S(1)} %get-tuple-element.9), channel_id=1, source_target_pairs={{0,3},{4,7},{8,11},{12,15},{16,19},{20,23},{24,27},{28,31},{32,35}... | collective-permute-start | bytes 393224 | tf_op jit(solution)/shard_map/ppermute | solution.py:197

commit v2 on v1

v2 whole, which is shorter than its diff:
```python
import functools

import jax
import jax.numpy as jnp
import numpy as np
from jax import lax
from jax.experimental import pallas as pl
from jax.experimental.pallas import tpu as pltpu
from jax.sharding import Mesh, PartitionSpec as P

FINE = ("x_lo", "z_hi", "z_lo", "y", "x_hi", "core")
SHAPE = (2, 2, 4, 8, 2, 2)
REGION = ("z_lo", "y", "x_hi", "core")
BF = jnp.bfloat16
F32 = jnp.float32


MIRROR_Y = True


def encoder(block, slab):
    x_lo, z_hi, z_lo, y = slab >> 6, (slab >> 5) & 1, (slab >> 3) & 3, slab & 7
    z_lo ^= 3 * (z_hi ^ (block & 1))
    y ^= 7 * z_hi * MIRROR_Y
    return (((block * 4 + z_lo) * 8 + y) * 2 + x_lo) * 2 + z_hi


PAIRS = [(b, s) for b in range(4) for s in range(128)]
REGION_ROUTE = [(s * 4 + b, encoder(b, s)) for b, s in PAIRS]
Z_ROUTE = [(encoder(b, s), encoder(b, s + 1)) for b, s in PAIRS if s < 127]
ZY_ROUTE = [(encoder(b, s), encoder(b + 1, s + 1)) for b, s in PAIRS if b < 3 and s < 127]
Y_ROUTE = [(encoder(b, s), encoder(b + 1, s)) for b, s in PAIRS if b < 3]
OUT_ROUTES = [[(encoder(b, s), s * 4 + (b ^ i)) for b, s in PAIRS] for i in range(4)]


def one_hots():
    own = np.zeros((2, 2, 2, 3, 3, 3, 4, 5, 3, 4, 4, 2), np.float32)
    halo = np.zeros((2, 2, 2, 3, 3, 3, 4, 5, 4, 4, 3, 2), np.float32)
    for n in range(2):
        for par in range(2):
            for ky in range(3):
                t, yy = (n, 1) if ky == 0 else (n + 1, ky - 1)
                for kx in range(3):
                    r = 2 * par + kx
                    for c in range(4):
                        for plane, kz, z in ((0, 1, 0), (0, 2, 1), (1, 0, 1), (1, 1, 2), (1, 2, 3)):
                            own[plane, n, par, kz, ky, kx, c, r, t, c, z, yy] = 1
                        for plane, kz, z in ((0, 0, 1), (0, 1, 2), (0, 2, 3), (1, 0, 3)):
                            halo[plane, n, par, kz, ky, kx, c, r, t, c, z - 1, yy] = 1
    return own.reshape(8, 108, 480), halo.reshape(8, 108, 480)


def dot(a, b):
    return jnp.dot(a, b, preferred_element_type=F32)


def one_hot(rows, columns, hit):
    row = lax.broadcasted_iota(jnp.int32, (rows, columns), 0)
    column = lax.broadcasted_iota(jnp.int32, (rows, columns), 1)
    return jnp.where(hit(row, column), 1.0, 0.0).astype(BF)


def next_cell():
    return one_hot(128, 128, lambda q, to: q + 1 == to)


def split_phases(place_ref, field_ref, out_ref, phases_ref):
    @pl.when(pl.program_id(0) == 0)
    def _():
        phases_ref[...] = one_hot(512, 512, lambda x, to: x == 4 * (to & 127) + (to >> 7))

    core = pl.program_id(0) & 1
    flips = 24 * (core ^ (place_ref[0] & 1)) + 7 * core * MIRROR_Y
    rows = dot(field_ref[...].reshape(256, 512), phases_ref[...])
    for k in range(32):
        out_ref[k ^ flips, 0] = rows[8 * k : 8 * k + 8].astype(BF)


def mask_rows(region_ref, rows_ref, masked_ref, halo_ref):
    upper = one_hot(48, 64, lambda row, source: source == row + 2 * ((row * 43) >> 8) + 2)
    for pair in range(16):
        keep = region_ref[0, pair].astype(F32).astype(BF)
        rows = rows_ref[64 * pair : 64 * pair + 64, :] * keep
        masked_ref[64 * pair : 64 * pair + 64, :] = rows
        halo_ref[48 * pair : 48 * pair + 48, :] = dot(upper, rows).astype(BF)


def operand(first, parts):
    return jnp.concatenate([first] + [part[:, 128 * r : 128 * r + 128] for r in range(4) for part in parts], 0)


def silu(v):
    half = 0.5 * v
    return half + half * jnp.tanh(half)


def hidden_planes(lower, upper, rows, bias, low_plane):
    planes = (lower[0:rows], upper[0:rows] + lower[128 : 128 + rows], upper[128 : 128 + rows])
    values = [silu(plane + bias[0:rows]) for plane in planes]
    return [values[0] * low_plane] + values[1:]


def latent_row(second_ref, taps):
    both = dot(second_ref[...], taps)
    lane = lax.broadcasted_iota(jnp.int32, (128, 128), 1)
    return both[0:128] + jnp.where(lane == 0, 0.0, pltpu.roll(both[128:256], 1, 1))


def encode(place_ref, own_ref, zed_ref, why_ref, both_ref, own_kernel_ref, halo_kernel_ref, bias_ref, second_ref, out_ref, own_first, zed_first, hidden, latent):
    block, slab = place_ref[0], place_ref[1]
    shift = next_cell()
    own_first[0:64, :] = dot(why_ref[:, 384:512], shift).astype(BF)
    own_first[64:1088, :] = dot(own_ref[:, 384:512], shift).astype(BF)
    zed_first[0:48, :] = dot(both_ref[:, 384:512], shift).astype(BF)
    zed_first[48:816, :] = dot(zed_ref[:, 384:512], shift).astype(BF)
    bias = bias_ref[...]
    low_plane = jnp.where(slab == 0, 0.0, 1.0).astype(F32)
    low_row = jnp.where(block == 0, 0.0, 1.0).astype(F32)
    for p in range(17):
        rows, own_rows, zed_rows = 128, 96, 96
        own_w, zed_w = own_kernel_ref[...], halo_kernel_ref[...]
        if p == 16:
            rows, own_rows, zed_rows = 64, 64, 48
            own_w = jnp.concatenate([own_w[:, 96 * r : 96 * r + 64] for r in range(5)], 1)
            zed_w = jnp.concatenate([zed_w[:, 96 * r : 96 * r + 48] for r in range(5)], 1)
        if p == 0:
            own_parts, zed_parts = [why_ref[...], own_ref[0:32, :]], [both_ref[...], zed_ref[0:48, :]]
        else:
            own_parts = [own_ref[64 * p - 64 : 64 * p - 64 + own_rows, :]]
            zed_parts = [zed_ref[48 * p - 48 : 48 * p - 48 + zed_rows, :]]
        upper = dot(own_w, operand(own_first[64 * p : 64 * p + own_rows, :], own_parts))
        lower = dot(zed_w, operand(zed_first[48 * p : 48 * p + zed_rows, :], zed_parts))
        for kz, value in enumerate(hidden_planes(lower, upper, rows, bias, low_plane)):
            if p == 0:
                value = jnp.concatenate([value[0:64] * low_row, value[64:128]], 0)
            hidden[kz, 128 * p : 128 * p + rows, :] = value.astype(BF)
    for o in range(16):
        taps = jnp.concatenate([hidden[kz, 128 * o : 128 * o + 192, :] for kz in range(3)], 0)
        latent[:, o, :] = latent_row(second_ref, taps)
    for g in range(4):
        out_ref[block ^ g] = latent[32 * g : 32 * g + 32].astype(BF)


def join_blocks(place_ref, a_ref, b_ref, c_ref, d_ref, out_ref):
    group = place_ref[0]
    for i, ref in enumerate((a_ref, b_ref, c_ref, d_ref)):
        start = pl.multiple_of((group ^ i) * 16, 16)
        out_ref[:, pl.ds(start, 16), :] = ref[...]


VMEM = pl.BlockSpec(memory_space=pltpu.VMEM)
SMEM = pl.BlockSpec(memory_space=pltpu.SMEM)
PARAMS = pltpu.CompilerParams(vmem_limit_bytes=32 * 1024 * 1024)


def body(field_rows, region, first_kernel, first_bias, second_kernel):
    own_hot, halo_hot = (jnp.asarray(a, BF) for a in one_hots())
    block = lax.axis_index("x_lo") * 2 + lax.axis_index("z_hi")
    inner = lax.axis_index("x_hi") * 2 + lax.axis_index("core")
    core = lax.axis_index("core")
    z_lo = lax.axis_index("z_lo") ^ (3 * (core ^ lax.axis_index("z_hi")))
    slab = inner * 32 + z_lo * 8 + (lax.axis_index("y") ^ (7 * core * MIRROR_Y))
    place = jnp.stack([block, slab]).astype(jnp.int32)

    keep = lax.ppermute(region, FINE, REGION_ROUTE)
    split = pl.pallas_call(
        split_phases,
        grid=(4,),
        in_specs=[SMEM, pl.BlockSpec((128, 2, 512), lambda i: (i, 0, 0))],
        out_specs=pl.BlockSpec((32, 1, 8, 512), lambda i: (0, i, 0, 0)),
        out_shape=jax.ShapeDtypeStruct((32, 4, 8, 512), BF),
        scratch_shapes=[pltpu.VMEM((512, 512), BF)],
        compiler_params=pltpu.CompilerParams(vmem_limit_bytes=60 * 1024 * 1024),
    )(place, field_rows.reshape(512, 2, 512))
    rows = lax.all_to_all(split.reshape(128, 8, 512), REGION, split_axis=0, concat_axis=0, tiled=True)
    taps = first_kernel.transpose(2, 3, 4, 1, 0).reshape(108, 32)
    own_kernel = jnp.einsum("kh,bkm->bhm", taps, own_hot, preferred_element_type=F32).astype(BF).reshape(256, 480)
    halo_kernel = jnp.einsum("kh,bkm->bhm", taps, halo_hot, preferred_element_type=F32).astype(BF).reshape(256, 480)
    bias = jnp.broadcast_to(jnp.tile(first_bias, 4)[:, None], (128, 128))
    second = second_kernel.transpose(0, 2, 3, 4, 1).reshape(128, 9, 3, 32)
    straight = second[:, :, 1:3].reshape(128, 576)
    earlier = jnp.pad(second[:, :, 0:1], ((0, 0), (0, 0), (1, 0), (0, 0))).reshape(128, 576)
    second = jnp.concatenate([straight, earlier], 0)

    rows, own_kernel, halo_kernel, bias, second = lax.optimization_barrier((rows, own_kernel, halo_kernel, bias, second))
    own, upper_rows = pl.pallas_call(
        mask_rows,
        in_specs=[SMEM, VMEM],
        out_specs=[VMEM, VMEM],
        out_shape=[jax.ShapeDtypeStruct((1024, 512), BF), jax.ShapeDtypeStruct((768, 512), BF)],
        compiler_params=PARAMS,
    )(keep, rows.reshape(1024, 512))
    zed = lax.ppermute(upper_rows, FINE, Z_ROUTE)
    why = lax.ppermute(own[960:1024], FINE, Y_ROUTE)
    both = lax.ppermute(upper_rows[720:768], FINE, ZY_ROUTE)
    pieces = pl.pallas_call(
        encode,
        in_specs=[SMEM] + [VMEM] * 8,
        out_specs=VMEM,
        out_shape=jax.ShapeDtypeStruct((4, 32, 16, 128), BF),
        scratch_shapes=[
            pltpu.VMEM((1088, 128), BF),
            pltpu.VMEM((816, 128), BF),
            pltpu.VMEM((3, 2112, 128), BF),
            pltpu.VMEM((128, 16, 128), F32),
        ],
        compiler_params=PARAMS,
    )(place, own, zed, why, both, own_kernel, halo_kernel, bias, second)
    moved = [lax.ppermute(pieces[i], FINE, OUT_ROUTES[i]) for i in range(4)]
    joined = pl.pallas_call(
        join_blocks,
        in_specs=[SMEM] + [VMEM] * 4,
        out_specs=VMEM,
        out_shape=jax.ShapeDtypeStruct((32, 64, 128), BF),
        compiler_params=PARAMS,
    )(inner.astype(jnp.int32).reshape(1), *moved)
    return joined.reshape(32, 1, 64, 128)


def solution(mesh):
    fine = Mesh(mesh.devices.reshape(SHAPE), FINE)
    slab, chan = FINE[:4], FINE[4:]
    in_specs = (P(chan, None, slab, None), P(slab, chan), P(), P(), P())
    out_specs = P(chan, slab, None, None)
    return jax.shard_map(body, mesh=fine, in_specs=in_specs, out_specs=out_specs, check_vma=False)
```

time: 118 us -> 105 us (0.89)
  the two profiles are of different devices: /device:TPU:2 before, /device:TPU:69 now
where the time goes in v2:
time: 105 us; the launch traced here: 104 us
  starting transfers between devices  62.2 us (59%)
  waiting for transfers between devices  27.5 us (26%)
  Pallas kernels  10.9 us (10%)
  local copies, waits for them, and re-layouts  2.07 us (2%)
    ppermute x4, starting transfers between devices, body(): moved = [lax.ppermute(pieces[i], FINE, OUT_ROUTES[i]) for i in range(4)]  25 us
    all_to_all x1, waiting for transfers between devices, body(): lax.all_to_all(split.reshape(128, 8, 512), REGION, split_axis=0, concat_a...  17.8 us
    all_to_all x1, starting transfers between devices, body(): lax.all_to_all(split.reshape(128, 8, 512), REGION, split_axis=0, concat_a...  16.5 us
    ppermute x1, starting transfers between devices, body(): keep = lax.ppermute(region, FINE, REGION_ROUTE)  7.52 us
    ppermute x4, waiting for transfers between devices, body(): moved = [lax.ppermute(pieces[i], FINE, OUT_ROUTES[i]) for i in range(4)]  7.35 us
    ppermute x1, starting transfers between devices, body(): why = lax.ppermute(own[960:1024], FINE, Y_ROUTE)  6.72 us
    pallas_call x1, Pallas kernels, body(): pl.pallas_call(encode, in_specs=[SMEM] + [VMEM] * 8, out_specs=VMEM, out_...  4.96 us
    ppermute x1, starting transfers between devices, body(): both = lax.ppermute(upper_rows[720:768], FINE, ZY_ROUTE)  4.58 us
  transfers between devices with their start and end apart: 9, of which 5 were waited for; matrix products, arithmetic and copies ran while one was open for 1% of the time, Pallas kernels for 0%

profile of v2, /device:TPU:69, one launch (start us, length us, event | category | flops | bytes accessed | tf_op | source)
XLA Modules:
  0.0 104.1 jit_solution(14481536236536582580)
XLA Ops:
  0.0 0.6 pad_add_fusion.place_ref
  0.6 4.1 %shard_map.73 = bf16[32,4,8,512]{3,2,1,0:T(8,128)(2,1)} custom-call(s32[2]{0:T(128)} %pad_add_fusion.place_ref, bf16[512,2,512]{2,1,0:T(2,128)(2,1)} %bitcast.41), custom_call_target="tpu_custom_call" | custom-call | tf_op jit(solution)/shard_map/pallas_call | solution.py:166
  4.8 16.5 %all-to-all-start = ((bf16[128,8,512]{2,1,0:T(8,128)(2,1)}), bf16[128,8,512]{2,1,0:T(8,128)(2,1)S(1)}, u32[]{:S(2)}, u32[]{:S(2)}) async-start(bf16[128,8,512]{2,1,0:T(8,128)(2,1)} %bitcast.40), calls=%async_computation | async-start | bytes 2097152 | tf_op jit(solution)/shard_map/all_to_all | solution.py:175
  21.3 7.5 %collective-permute-start = (s32[1,16]{1,0:T(1,128)S(1)}, s32[1,16]{1,0:T(1,128)S(1)}, u32[]{:S(2)}, u32[]{:S(2)}) collective-permute-start(s32[1,16]{1,0:T(1,128)S(1)} %copy-done.6), channel_id=1, source_target_pairs={{0,0},{4,4},{8,8},{12,12},{16,16},{20,20},{24,24},{28,28},{32,32},... | collective-permute-start | bytes 200 | tf_op jit(solution)/shard_map/ppermute | solution.py:165
  28.9 0.6 copy-done.5
  29.8 0.2 copy.15
  30.0 0.3 convolution_convert_fusion
  30.3 0.8 copy-done.1
  31.1 0.3 convolution_convert_fusion.1
  31.4 17.8 %all-to-all-done = bf16[128,8,512]{2,1,0:T(8,128)(2,1)S(1)} async-done(((bf16[128,8,512]{2,1,0:T(8,128)(2,1)}), bf16[128,8,512]{2,1,0:T(8,128)(2,1)S(1)}, u32[]{:S(2)}, u32[]{:S(2)}) %all-to-all-start) | async-done | bytes 1048608 | tf_op jit(solution)/shard_map/all_to_all | solution.py:175
  49.3 1.2 %collective-permute-done.region_ref = s32[1,16]{1,0:T(1,128)S(1)} collective-permute-done((s32[1,16]{1,0:T(1,128)S(1)}, s32[1,16]{1,0:T(1,128)S(1)}, u32[]{:S(2)}, u32[]{:S(2)}) %collective-permute-start) | collective-permute-done | bytes 96 | tf_op jit(solution)/shard_map/ppermute | solution.py:165
  50.5 0.9 shard_map.74
  51.4 1.9 %collective-permute-start.1 = (bf16[768,512]{1,0:T(8,128)(2,1)S(1)}, bf16[768,512]{1,0:T(8,128)(2,1)S(1)}, u32[]{:S(2)}, u32[]{:S(2)}) collective-permute-start(bf16[768,512]{1,0:T(8,128)(2,1)S(1)} %get-tuple-element.14), channel_id=1, source_target_pairs={{0,4},{4,8},{8,12},{12,16},{16,20},{20,24},{24,28},{28,32},{32,36}... | collective-permute-start | bytes 2359304 | tf_op jit(solution)/shard_map/ppermute | solution.py:193
  53.3 6.7 %collective-permute-start.2 = (bf16[64,512]{1,0:T(8,128)(2,1)S(1)}, bf16[64,512]{1,0:T(8,128)(2,1)S(1)}, u32[]{:S(2)}, u32[]{:S(2)}) collective-permute-start(bf16[64,512]{1,0:T(8,128)(2,1)S(1)} %slice.26), channel_id=1, source_target_pairs={{0,224},{4,228},{8,232},{12,236},{16,240},{20,244},{24,248},{28,25... | collective-permute-start | bytes 196616 | tf_op jit(solution)/shard_map/ppermute | solution.py:194
  60.1 4.6 %collective-permute-start.3 = (bf16[48,512]{1,0:T(8,128)(2,1)S(1)}, bf16[48,512]{1,0:T(8,128)(2,1)S(1)}, u32[]{:S(2)}, u32[]{:S(2)}) collective-permute-start(bf16[48,512]{1,0:T(8,128)(2,1)S(1)} %slice.27), channel_id=1, source_target_pairs={{0,228},{4,232},{8,236},{12,240},{16,244},{20,248},{24,252},{28,19... | collective-permute-start | bytes 147464 | tf_op jit(solution)/shard_map/ppermute | solution.py:195
  64.7 1.2 %collective-permute-done.3.both_ref = bf16[48,512]{1,0:T(8,128)(2,1)S(1)} collective-permute-done((bf16[48,512]{1,0:T(8,128)(2,1)S(1)}, bf16[48,512]{1,0:T(8,128)(2,1)S(1)}, u32[]{:S(2)}, u32[]{:S(2)}) %collective-permute-start.3) | collective-permute-done | bytes 49184 | tf_op jit(solution)/shard_map/ppermute | solution.py:195
  65.8 5.0 %shard_map.75 = bf16[4,32,16,128]{3,2,1,0:T(8,128)(2,1)S(1)} custom-call(s32[2]{0:T(128)S(1)} %copy-done, bf16[1024,512]{1,0:T(8,128)(2,1)S(1)} %get-tuple-element.13.own_ref, bf16[768,512]{1,0:T(8,128)(2,1)S(1)} %collective-permute-done.1.zed_ref, bf16[64,512]{1,0:T(8,128)(2,1)S(1)} %collective-permute-done.2.why_ref, ...), custom_call_target="tpu_custom_call" | custom-call | tf_op jit(solution)/shard_map/pallas_call | solution.py:196
  70.9 9.2 %collective-permute-start.7 = (bf16[32,16,128]{2,1,0:T(8,128)(2,1)S(1)}, bf16[32,16,128]{2,1,0:T(8,128)(2,1)S(1)}, u32[]{:S(2)}, u32[]{:S(2)}) collective-permute-start(bf16[32,16,128]{2,1,0:T(8,128)(2,1)S(1)} %get-tuple-element.19), channel_id=1, source_target_pairs={{0,3},{4,7},{8,11},{12,15},{16,19},{20,23},{24,27},{28,31},{32,35}... | collective-permute-start | bytes 393224 | tf_op jit(solution)/shard_map/ppermute | solution.py:209
  80.1 11.1 %collective-permute-start.6 = (bf16[32,16,128]{2,1,0:T(8,128)(2,1)S(1)}, bf16[32,16,128]{2,1,0:T(8,128)(2,1)S(1)}, u32[]{:S(2)}, u32[]{:S(2)}) collective-permute-start(bf16[32,16,128]{2,1,0:T(8,128)(2,1)S(1)} %get-tuple-element.20), channel_id=1, source_target_pairs={{0,2},{4,6},{8,10},{12,14},{16,18},{20,22},{24,26},{28,30},{32,34}... | collective-permute-start | bytes 393224 | tf_op jit(solution)/shard_map/ppermute | solution.py:209
  91.1 1.9 %collective-permute-start.5 = (bf16[32,16,128]{2,1,0:T(8,128)(2,1)S(1)}, bf16[32,16,128]{2,1,0:T(8,128)(2,1)S(1)}, u32[]{:S(2)}, u32[]{:S(2)}) collective-permute-start(bf16[32,16,128]{2,1,0:T(8,128)(2,1)S(1)} %get-tuple-element.21), channel_id=1, source_target_pairs={{0,1},{4,5},{8,9},{12,13},{16,17},{20,21},{24,25},{28,29},{32,33},... | collective-permute-start | bytes 393224 | tf_op jit(solution)/shard_map/ppermute | solution.py:209
  93.1 2.8 %collective-permute-start.4 = (bf16[32,16,128]{2,1,0:T(8,128)(2,1)S(1)}, bf16[32,16,128]{2,1,0:T(8,128)(2,1)S(1)}, u32[]{:S(2)}, u32[]{:S(2)}) collective-permute-start(bf16[32,16,128]{2,1,0:T(8,128)(2,1)S(1)} %get-tuple-element.22), channel_id=1, source_target_pairs={{0,0},{4,4},{8,8},{12,12},{16,16},{20,20},{24,24},{28,28},{32,32},... | collective-permute-start | bytes 393224 | tf_op jit(solution)/shard_map/ppermute | solution.py:209
  95.9 1.5 %collective-permute-done.5.b_ref = bf16[32,16,128]{2,1,0:T(8,128)(2,1)S(1)} collective-permute-done((bf16[32,16,128]{2,1,0:T(8,128)(2,1)S(1)}, bf16[32,16,128]{2,1,0:T(8,128)(2,1)S(1)}, u32[]{:S(2)}, u32[]{:S(2)}) %collective-permute-start.5) | collective-permute-done | bytes 131104 | tf_op jit(solution)/shard_map/ppermute | solution.py:209
  97.4 5.8 %collective-permute-done.4.a_ref = bf16[32,16,128]{2,1,0:T(8,128)(2,1)S(1)} collective-permute-done((bf16[32,16,128]{2,1,0:T(8,128)(2,1)S(1)}, bf16[32,16,128]{2,1,0:T(8,128)(2,1)S(1)}, u32[]{:S(2)}, u32[]{:S(2)}) %collective-permute-start.4) | collective-permute-done | bytes 131104 | tf_op jit(solution)/shard_map/ppermute | solution.py:209
  103.2 0.9 shard_map.76
  (28 shorter events, 0.5 us)
Async XLA Ops:
  4.7 16.5 %copy-start.6 = (s32[1,16]{1,0:T(1,128)S(1)}, s32[1,16]{1,0:T(1,128)}, u32[]{:S(2)}) copy-start(s32[1,16]{1,0:T(1,128)} %param.8) | copy-start | bytes 196
  4.8 24.0 %copy-start.3 = (bf16[128,32,3,3,3]{0,1,4,3,2:T(8,128)(2,1)S(1)}, bf16[128,32,3,3,3]{0,1,4,3,2:T(8,128)(2,1)}, u32[]{:S(2)}) copy-start(bf16[128,32,3,3,3]{0,1,4,3,2:T(8,128)(2,1)} %param.11) | copy-start | bytes 663556
  4.8 44.5 %all-to-all-start = ((bf16[128,8,512]{2,1,0:T(8,128)(2,1)}), bf16[128,8,512]{2,1,0:T(8,128)(2,1)S(1)}, u32[]{:S(2)}, u32[]{:S(2)}) async-start(bf16[128,8,512]{2,1,0:T(8,128)(2,1)} %bitcast.40), calls=%async_computation | async-start | bytes 2097152 | tf_op jit(solution)/shard_map/all_to_all | solution.py:175
  21.3 29.2 %collective-permute-start = (s32[1,16]{1,0:T(1,128)S(1)}, s32[1,16]{1,0:T(1,128)S(1)}, u32[]{:S(2)}, u32[]{:S(2)}) collective-permute-start(s32[1,16]{1,0:T(1,128)S(1)} %copy-done.6), channel_id=1, source_target_pairs={{0,0},{4,4},{8,8},{12,12},{16,16},{20,20},{24,24},{28,28},{32,32},... | collective-permute-start | bytes 200 | tf_op jit(solution)/shard_map/ppermute | solution.py:165
  28.8 0.7 copy-start.5
  28.8 0.8 copy-start.4
  28.8 1.2 %copy-start.2 = (bf16[8,108,480]{2,1,0:T(8,128)(2,1)S(1)}, bf16[8,108,480]{2,1,0:T(8,128)(2,1)}, u32[]{:S(2)}) copy-start(bf16[8,108,480]{2,1,0:T(8,128)(2,1)} %constant.42.clone) | copy-start | bytes 2488324
  29.9 1.2 %copy-start.1 = (bf16[8,108,480]{2,1,0:T(8,128)(2,1)S(1)}, bf16[8,108,480]{2,1,0:T(8,128)(2,1)}, u32[]{:S(2)}) copy-start(bf16[8,108,480]{2,1,0:T(8,128)(2,1)} %constant.41.clone) | copy-start | bytes 2488324
  51.4 14.4 %collective-permute-start.1 = (bf16[768,512]{1,0:T(8,128)(2,1)S(1)}, bf16[768,512]{1,0:T(8,128)(2,1)S(1)}, u32[]{:S(2)}, u32[]{:S(2)}) collective-permute-start(bf16[768,512]{1,0:T(8,128)(2,1)S(1)} %get-tuple-element.14), channel_id=1, source_target_pairs={{0,4},{4,8},{8,12},{12,16},{16,20},{20,24},{24,28},{28,32},{32,36}... | collective-permute-start | bytes 2359304 | tf_op jit(solution)/shard_map/ppermute | solution.py:193
  53.3 12.5 %copy-start = (s32[2]{0:T(128)S(1)}, s32[2]{0:T(128)}, u32[]{:S(2)}) copy-start(s32[2]{0:T(128)} %pad_add_fusion.place_ref) | copy-start | bytes 28
  53.3 12.5 %collective-permute-start.2 = (bf16[64,512]{1,0:T(8,128)(2,1)S(1)}, bf16[64,512]{1,0:T(8,128)(2,1)S(1)}, u32[]{:S(2)}, u32[]{:S(2)}) collective-permute-start(bf16[64,512]{1,0:T(8,128)(2,1)S(1)} %slice.26), channel_id=1, source_target_pairs={{0,224},{4,228},{8,232},{12,236},{16,240},{20,244},{24,248},{28,25... | collective-permute-start | bytes 196616 | tf_op jit(solution)/shard_map/ppermute | solution.py:194
  60.1 5.7 %collective-permute-start.3 = (bf16[48,512]{1,0:T(8,128)(2,1)S(1)}, bf16[48,512]{1,0:T(8,128)(2,1)S(1)}, u32[]{:S(2)}, u32[]{:S(2)}) collective-permute-start(bf16[48,512]{1,0:T(8,128)(2,1)S(1)} %slice.27), channel_id=1, source_target_pairs={{0,228},{4,232},{8,236},{12,240},{16,244},{20,248},{24,252},{28,19... | collective-permute-start | bytes 147464 | tf_op jit(solution)/shard_map/ppermute | solution.py:195
  70.9 25.0 %collective-permute-start.7 = (bf16[32,16,128]{2,1,0:T(8,128)(2,1)S(1)}, bf16[32,16,128]{2,1,0:T(8,128)(2,1)S(1)}, u32[]{:S(2)}, u32[]{:S(2)}) collective-permute-start(bf16[32,16,128]{2,1,0:T(8,128)(2,1)S(1)} %get-tuple-element.19), channel_id=1, source_target_pairs={{0,3},{4,7},{8,11},{12,15},{16,19},{20,23},{24,27},{28,31},{32,35}... | collective-permute-start | bytes 393224 | tf_op jit(solution)/shard_map/ppermute | solution.py:209
  80.1 15.8 %collective-permute-start.6 = (bf16[32,16,128]{2,1,0:T(8,128)(2,1)S(1)}, bf16[32,16,128]{2,1,0:T(8,128)(2,1)S(1)}, u32[]{:S(2)}, u32[]{:S(2)}) collective-permute-start(bf16[32,16,128]{2,1,0:T(8,128)(2,1)S(1)} %get-tuple-element.20), channel_id=1, source_target_pairs={{0,2},{4,6},{8,10},{12,14},{16,18},{20,22},{24,26},{28,30},{32,34}... | collective-permute-start | bytes 393224 | tf_op jit(solution)/shard_map/ppermute | solution.py:209
  91.1 6.3 %collective-permute-start.5 = (bf16[32,16,128]{2,1,0:T(8,128)(2,1)S(1)}, bf16[32,16,128]{2,1,0:T(8,128)(2,1)S(1)}, u32[]{:S(2)}, u32[]{:S(2)}) collective-permute-start(bf16[32,16,128]{2,1,0:T(8,128)(2,1)S(1)} %get-tuple-element.21), channel_id=1, source_target_pairs={{0,1},{4,5},{8,9},{12,13},{16,17},{20,21},{24,25},{28,29},{32,33},... | collective-permute-start | bytes 393224 | tf_op jit(solution)/shard_map/ppermute | solution.py:209
  93.1 10.2 %collective-permute-start.4 = (bf16[32,16,128]{2,1,0:T(8,128)(2,1)S(1)}, bf16[32,16,128]{2,1,0:T(8,128)(2,1)S(1)}, u32[]{:S(2)}, u32[]{:S(2)}) collective-permute-start(bf16[32,16,128]{2,1,0:T(8,128)(2,1)S(1)} %get-tuple-element.22), channel_id=1, source_target_pairs={{0,0},{4,4},{8,8},{12,12},{16,16},{20,20},{24,24},{28,28},{32,32},... | collective-permute-start | bytes 393224 | tf_op jit(solution)/shard_map/ppermute | solution.py:209

commit v3 on v2

--- a/solution.py
+++ b/solution.py
@@ -30,7 +30,8 @@
 Z_ROUTE = [(encoder(b, s), encoder(b, s + 1)) for b, s in PAIRS if s < 127]
 ZY_ROUTE = [(encoder(b, s), encoder(b + 1, s + 1)) for b, s in PAIRS if b < 3 and s < 127]
 Y_ROUTE = [(encoder(b, s), encoder(b + 1, s)) for b, s in PAIRS if b < 3]
-OUT_ROUTES = [[(encoder(b, s), s * 4 + (b ^ i)) for b, s in PAIRS] for i in range(4)]
+OUT_ROUTES = [[(encoder(b, s), s * 4 + (b ^ i)) for b, s in PAIRS] for i in (0, 2)]
+CORE_ROUTE = [(i, i ^ 1) for i in range(512)]
 
 
 def one_hots():
@@ -64,13 +65,13 @@
     return one_hot(128, 128, lambda q, to: q + 1 == to)
 
 
-def split_phases(place_ref, field_ref, out_ref, phases_ref):
+def split_phases(field_ref, out_ref, phases_ref):
     @pl.when(pl.program_id(0) == 0)
     def _():
         phases_ref[...] = one_hot(512, 512, lambda x, to: x == 4 * (to & 127) + (to >> 7))
 
     core = pl.program_id(0) & 1
-    flips = 24 * (core ^ (place_ref[0] & 1)) + 7 * core * MIRROR_Y
+    flips = 24 * (core ^ lax.axis_index("z_hi")) + 7 * core * MIRROR_Y
     rows = dot(field_ref[...].reshape(256, 512), phases_ref[...])
     for k in range(32):
         out_ref[k ^ flips, 0] = rows[8 * k : 8 * k + 8].astype(BF)
@@ -138,14 +139,17 @@
         taps = jnp.concatenate([hidden[kz, 128 * o : 128 * o + 192, :] for kz in range(3)], 0)
         latent[:, o, :] = latent_row(second_ref, taps)
     for g in range(4):
-        out_ref[block ^ g] = latent[32 * g : 32 * g + 32].astype(BF)
-
-
-def join_blocks(place_ref, a_ref, b_ref, c_ref, d_ref, out_ref):
+        out_ref[(block & 2) ^ g] = latent[32 * g : 32 * g + 32].astype(BF)
+
+
+def join_blocks(place_ref, a_ref, b_ref, other_ref, out_ref):
     group = place_ref[0]
-    for i, ref in enumerate((a_ref, b_ref, c_ref, d_ref)):
-        start = pl.multiple_of((group ^ i) * 16, 16)
-        out_ref[:, pl.ds(start, 16), :] = ref[...]
+    core = group & 1
+    for i, ref in enumerate((a_ref, b_ref)):
+        near = pl.multiple_of((group ^ (2 * i)) * 16, 16)
+        out_ref[:, pl.ds(near, 16), :] = ref[core]
+        far = pl.multiple_of((group ^ (2 * i + 1)) * 16, 16)
+        out_ref[:, pl.ds(far, 16), :] = other_ref[i]
 
 
 VMEM = pl.BlockSpec(memory_space=pltpu.VMEM)
@@ -166,12 +170,12 @@
     split = pl.pallas_call(
         split_phases,
         grid=(4,),
-        in_specs=[SMEM, pl.BlockSpec((128, 2, 512), lambda i: (i, 0, 0))],
+        in_specs=[pl.BlockSpec((128, 2, 512), lambda i: (i, 0, 0))],
         out_specs=pl.BlockSpec((32, 1, 8, 512), lambda i: (0, i, 0, 0)),
         out_shape=jax.ShapeDtypeStruct((32, 4, 8, 512), BF),
         scratch_shapes=[pltpu.VMEM((512, 512), BF)],
         compiler_params=pltpu.CompilerParams(vmem_limit_bytes=60 * 1024 * 1024),
-    )(place, field_rows.reshape(512, 2, 512))
+    )(field_rows.reshape(512, 2, 512))
     rows = lax.all_to_all(split.reshape(128, 8, 512), REGION, split_axis=0, concat_axis=0, tiled=True)
     taps = first_kernel.transpose(2, 3, 4, 1, 0).reshape(108, 32)
     own_kernel = jnp.einsum("kh,bkm->bhm", taps, own_hot, preferred_element_type=F32).astype(BF).reshape(256, 480)
@@ -206,14 +210,16 @@
         ],
         compiler_params=PARAMS,
     )(place, own, zed, why, both, own_kernel, halo_kernel, bias, second)
-    moved = [lax.ppermute(pieces[i], FINE, OUT_ROUTES[i]) for i in range(4)]
+    a, b = (lax.ppermute(pieces[2 * i : 2 * i + 2], FINE, OUT_ROUTES[i]) for i in range(2))
+    away = jnp.stack([lax.dynamic_index_in_dim(v, 1 - core, 0, keepdims=False) for v in (a, b)])
+    other = lax.ppermute(away, FINE, CORE_ROUTE)
     joined = pl.pallas_call(
         join_blocks,
-        in_specs=[SMEM] + [VMEM] * 4,
+        in_specs=[SMEM] + [VMEM] * 3,
         out_specs=VMEM,
         out_shape=jax.ShapeDtypeStruct((32, 64, 128), BF),
         compiler_params=PARAMS,
-    )(inner.astype(jnp.int32).reshape(1), *moved)
+    )(inner.astype(jnp.int32).reshape(1), a, b, other)
     return joined.reshape(32, 1, 64, 128)
 
 

time: 105 us -> 103 us (0.981)
  the two profiles are of different devices: /device:TPU:69 before, /device:TPU:321 now
where the time goes in v3:
time: 103 us
  starting transfers between devices  49.4 us (48%)
  waiting for transfers between devices  37.5 us (36%)
  Pallas kernels  11.6 us (11%)
  local copies, waits for them, and re-layouts  2.09 us (2%)
  matrix products  1.85 us (2%)
    all_to_all x1, waiting for transfers between devices, body(): lax.all_to_all(split.reshape(128, 8, 512), REGION, split_axis=0, concat_a...  21.4 us
    all_to_all x1, starting transfers between devices, body(): lax.all_to_all(split.reshape(128, 8, 512), REGION, split_axis=0, concat_a...  14.7 us
    ppermute x1, starting transfers between devices, body(): other = lax.ppermute(away, FINE, CORE_ROUTE)  10.2 us
    ppermute x2, waiting for transfers between devices, body(): lax.ppermute(pieces[2 * i:2 * i + 2], FINE, OUT_ROUTES[i])  9.36 us
    ppermute x2, starting transfers between devices, body(): lax.ppermute(pieces[2 * i:2 * i + 2], FINE, OUT_ROUTES[i])  8.06 us
    ppermute x1, starting transfers between devices, body(): both = lax.ppermute(upper_rows[720:768], FINE, ZY_ROUTE)  5.66 us
    pallas_call x1, Pallas kernels, body(): pl.pallas_call(encode, in_specs=[SMEM] + [VMEM] * 8, out_specs=VMEM, out_...  4.82 us
    ppermute x1, starting transfers between devices, body(): keep = lax.ppermute(region, FINE, REGION_ROUTE)  4.49 us
  transfers between devices with their start and end apart: 8, of which 6 were waited for; matrix products, arithmetic and copies ran while one was open for 3% of the time, Pallas kernels for 0%

profile of v3, /device:TPU:321, one launch (start us, length us, event | category | flops | bytes accessed | tf_op | source)
XLA Modules:
  0.0 102.8 jit_solution(5012502314140639095)
XLA Ops:
  0.0 4.1 %shard_map.73 = bf16[32,4,8,512]{3,2,1,0:T(8,128)(2,1)} custom-call(bf16[512,2,512]{2,1,0:T(2,128)(2,1)} %bitcast.33), custom_call_target="tpu_custom_call" | custom-call | tf_op jit(solution)/shard_map/pallas_call | solution.py:170
  4.1 14.7 %all-to-all-start = ((bf16[128,8,512]{2,1,0:T(8,128)(2,1)}), bf16[128,8,512]{2,1,0:T(8,128)(2,1)S(1)}, u32[]{:S(2)}, u32[]{:S(2)}) async-start(bf16[128,8,512]{2,1,0:T(8,128)(2,1)} %bitcast.32), calls=%async_computation | async-start | bytes 2097152 | tf_op jit(solution)/shard_map/all_to_all | solution.py:179
  18.8 4.5 %collective-permute-start = (s32[1,16]{1,0:T(1,128)S(1)}, s32[1,16]{1,0:T(1,128)S(1)}, u32[]{:S(2)}, u32[]{:S(2)}) collective-permute-start(s32[1,16]{1,0:T(1,128)S(1)} %copy-done.4), channel_id=1, source_target_pairs={{0,0},{4,4},{8,8},{12,12},{16,16},{20,20},{24,24},{28,28},{32,32},... | collective-permute-start | bytes 200 | tf_op jit(solution)/shard_map/ppermute | solution.py:169
  23.4 0.6 copy-done.3
  24.2 0.2 copy.16
  24.3 0.2 copy.15
  24.6 1.6 %convolution_convert_fusion = bf16[8,480,32]{1,2,0:T(8,128)(2,1)S(1)} fusion(bf16[8,108,480]{2,1,0:T(8,128)(2,1)} %constant.52.clone, bf16[108,32]{1,0:T(8,128)(2,1)S(1)} %reshape.38), kind=kOutput, calls=%fused_computation | convolution fusion | flops 26664960 | bytes 1082112 | tf_op jit(solution)/shard_map/kh,bkm->bhm/dot_general | solution.py:182
  26.1 0.3 convolution_convert_fusion.1
  26.4 21.4 %all-to-all-done = bf16[128,8,512]{2,1,0:T(8,128)(2,1)S(1)} async-done(((bf16[128,8,512]{2,1,0:T(8,128)(2,1)}), bf16[128,8,512]{2,1,0:T(8,128)(2,1)S(1)}, u32[]{:S(2)}, u32[]{:S(2)}) %all-to-all-start) | async-done | bytes 1048608 | tf_op jit(solution)/shard_map/all_to_all | solution.py:179
  48.0 1.8 %shard_map.74 = (bf16[1024,512]{1,0:T(8,128)(2,1)S(1)}, bf16[768,512]{1,0:T(8,128)(2,1)}) custom-call(s32[1,16]{1,0:T(1,128)S(1)} %collective-permute-done.region_ref, bf16[1024,512]{1,0:T(8,128)(2,1)S(1)} %bitcast.29), custom_call_target="tpu_custom_call" | custom-call | tf_op jit(solution)/shard_map/pallas_call | solution.py:190
  49.8 3.4 %collective-permute-start.1 = (bf16[768,512]{1,0:T(8,128)(2,1)}, bf16[768,512]{1,0:T(8,128)(2,1)S(1)}, u32[]{:S(2)}, u32[]{:S(2)}) collective-permute-start(bf16[768,512]{1,0:T(8,128)(2,1)} %get-tuple-element.14), channel_id=1, source_target_pairs={{0,4},{4,8},{8,12},{12,16},{16,20},{20,24},{24,28},{28,32},{32,36}... | collective-permute-start | bytes 2359304 | tf_op jit(solution)/shard_map/ppermute | solution.py:197
  53.2 0.8 slice.21
  54.0 5.7 %collective-permute-start.3 = (bf16[48,512]{1,0:T(8,128)(2,1)S(1)}, bf16[48,512]{1,0:T(8,128)(2,1)S(1)}, u32[]{:S(2)}, u32[]{:S(2)}) collective-permute-start(bf16[48,512]{1,0:T(8,128)(2,1)S(1)} %slice.21), channel_id=1, source_target_pairs={{0,228},{4,232},{8,236},{12,240},{16,244},{20,248},{24,252},{28,19... | collective-permute-start | bytes 147464 | tf_op jit(solution)/shard_map/ppermute | solution.py:199
  59.7 2.8 %collective-permute-start.2 = (bf16[64,512]{1,0:T(8,128)(2,1)S(1)}, bf16[64,512]{1,0:T(8,128)(2,1)S(1)}, u32[]{:S(2)}, u32[]{:S(2)}) collective-permute-start(bf16[64,512]{1,0:T(8,128)(2,1)S(1)} %slice.20), channel_id=1, source_target_pairs={{0,224},{4,228},{8,232},{12,236},{16,240},{20,244},{24,248},{28,25... | collective-permute-start | bytes 196616 | tf_op jit(solution)/shard_map/ppermute | solution.py:198
  62.6 1.5 %collective-permute-done.3.both_ref = bf16[48,512]{1,0:T(8,128)(2,1)S(1)} collective-permute-done((bf16[48,512]{1,0:T(8,128)(2,1)S(1)}, bf16[48,512]{1,0:T(8,128)(2,1)S(1)}, u32[]{:S(2)}, u32[]{:S(2)}) %collective-permute-start.3) | collective-permute-done | bytes 49184 | tf_op jit(solution)/shard_map/ppermute | solution.py:199
  64.1 4.1 %collective-permute-done.2.why_ref = bf16[64,512]{1,0:T(8,128)(2,1)S(1)} collective-permute-done((bf16[64,512]{1,0:T(8,128)(2,1)S(1)}, bf16[64,512]{1,0:T(8,128)(2,1)S(1)}, u32[]{:S(2)}, u32[]{:S(2)}) %collective-permute-start.2) | collective-permute-done | bytes 65568 | tf_op jit(solution)/shard_map/ppermute | solution.py:198
  68.2 4.8 %shard_map.75 = bf16[4,32,16,128]{3,2,1,0:T(8,128)(2,1)S(1)} custom-call(s32[2]{0:T(128)S(1)} %pad_add_fusion.place_ref, bf16[1024,512]{1,0:T(8,128)(2,1)S(1)} %get-tuple-element.13.own_ref, bf16[768,512]{1,0:T(8,128)(2,1)S(1)} %collective-permute-done.1.zed_ref, bf16[64,512]{1,0:T(8,128)(2,1)S(1)} %collective-permute-done.2.why_ref, ...), custom_call_target="tpu_custom_call" | custom-call | tf_op jit(solution)/shard_map/pallas_call | solution.py:200
  73.0 3.5 %collective-permute-start.5 = (bf16[2,32,16,128]{3,2,1,0:T(8,128)(2,1)S(1)}, bf16[2,32,16,128]{3,2,1,0:T(8,128)(2,1)S(1)}, u32[]{:S(2)}, u32[]{:S(2)}) collective-permute-start(bf16[2,32,16,128]{3,2,1,0:T(8,128)(2,1)S(1)} %get-tuple-element.19), channel_id=1, source_target_pairs={{0,2},{4,6},{8,10},{12,14},{16,18},{20,22},{24,26},{28,30},{32,34}... | collective-permute-start | bytes 786440 | tf_op jit(solution)/shard_map/ppermute | solution.py:213
  76.5 4.6 %collective-permute-start.4 = (bf16[2,32,16,128]{3,2,1,0:T(8,128)(2,1)S(1)}, bf16[2,32,16,128]{3,2,1,0:T(8,128)(2,1)S(1)}, u32[]{:S(2)}, u32[]{:S(2)}) collective-permute-start(bf16[2,32,16,128]{3,2,1,0:T(8,128)(2,1)S(1)} %get-tuple-element.20), channel_id=1, source_target_pairs={{0,0},{4,4},{8,8},{12,12},{16,16},{20,20},{24,24},{28,28},{32,32},... | collective-permute-start | bytes 786440 | tf_op jit(solution)/shard_map/ppermute | solution.py:213
  81.1 5.7 %collective-permute-done.5.b_ref = bf16[2,32,16,128]{3,2,1,0:T(8,128)(2,1)S(1)} collective-permute-done((bf16[2,32,16,128]{3,2,1,0:T(8,128)(2,1)S(1)}, bf16[2,32,16,128]{3,2,1,0:T(8,128)(2,1)S(1)}, u32[]{:S(2)}, u32[]{:S(2)}) %collective-permute-start.5) | collective-permute-done | bytes 262176 | tf_op jit(solution)/shard_map/ppermute | solution.py:213
  86.8 3.7 %collective-permute-done.4.a_ref = bf16[2,32,16,128]{3,2,1,0:T(8,128)(2,1)S(1)} collective-permute-done((bf16[2,32,16,128]{3,2,1,0:T(8,128)(2,1)S(1)}, bf16[2,32,16,128]{3,2,1,0:T(8,128)(2,1)S(1)}, u32[]{:S(2)}, u32[]{:S(2)}) %collective-permute-start.4) | collective-permute-done | bytes 262176 | tf_op jit(solution)/shard_map/ppermute | solution.py:213
  90.5 10.2 %collective-permute-start.6 = (bf16[2,32,16,128]{3,2,1,0:T(8,128)(2,1)S(1)}, bf16[2,32,16,128]{3,2,1,0:T(8,128)(2,1)S(1)}, u32[]{:S(2)}, u32[]{:S(2)}) collective-permute-start(bf16[2,32,16,128]{3,2,1,0:T(8,128)(2,1)S(1)} %pad_maximum_fusion.1), channel_id=1, source_target_pairs={{0,1},{1,0},{2,3},{3,2},{4,5},{5,4},{6,7},{7,6},{8,9},{9,8},{10,11... | collective-permute-start | bytes 786440 | tf_op jit(solution)/shard_map/ppermute | solution.py:215
  100.8 1.1 %collective-permute-done.6.other_ref = bf16[2,32,16,128]{3,2,1,0:T(8,128)(2,1)S(1)} collective-permute-done((bf16[2,32,16,128]{3,2,1,0:T(8,128)(2,1)S(1)}, bf16[2,32,16,128]{3,2,1,0:T(8,128)(2,1)S(1)}, u32[]{:S(2)}, u32[]{:S(2)}) %collective-permute-start.6) | collective-permute-done | bytes 262176 | tf_op jit(solution)/shard_map/ppermute | solution.py:215
  101.9 0.9 shard_map.76
  (25 shorter events, 0.5 us)
Async XLA Ops:
  4.1 14.7 %copy-start.4 = (s32[1,16]{1,0:T(1,128)S(1)}, s32[1,16]{1,0:T(1,128)}, u32[]{:S(2)}) copy-start(s32[1,16]{1,0:T(1,128)} %param.8) | copy-start | bytes 196
  4.1 19.2 %copy-start.1 = (bf16[128,32,3,3,3]{0,1,4,3,2:T(8,128)(2,1)S(1)}, bf16[128,32,3,3,3]{0,1,4,3,2:T(8,128)(2,1)}, u32[]{:S(2)}) copy-start(bf16[128,32,3,3,3]{0,1,4,3,2:T(8,128)(2,1)} %param.11) | copy-start | bytes 663556
  4.1 43.8 %all-to-all-start = ((bf16[128,8,512]{2,1,0:T(8,128)(2,1)}), bf16[128,8,512]{2,1,0:T(8,128)(2,1)S(1)}, u32[]{:S(2)}, u32[]{:S(2)}) async-start(bf16[128,8,512]{2,1,0:T(8,128)(2,1)} %bitcast.32), calls=%async_computation | async-start | bytes 2097152 | tf_op jit(solution)/shard_map/all_to_all | solution.py:179
  18.8 29.1 %collective-permute-start = (s32[1,16]{1,0:T(1,128)S(1)}, s32[1,16]{1,0:T(1,128)S(1)}, u32[]{:S(2)}, u32[]{:S(2)}) collective-permute-start(s32[1,16]{1,0:T(1,128)S(1)} %copy-done.4), channel_id=1, source_target_pairs={{0,0},{4,4},{8,8},{12,12},{16,16},{20,20},{24,24},{28,28},{32,32},... | collective-permute-start | bytes 200 | tf_op jit(solution)/shard_map/ppermute | solution.py:169
  23.4 0.7 copy-start.3
  23.4 0.8 copy-start.2
  24.5 1.6 %copy-start = (bf16[8,108,480]{2,1,0:T(8,128)(2,1)S(1)}, bf16[8,108,480]{2,1,0:T(8,128)(2,1)}, u32[]{:S(2)}) copy-start(bf16[8,108,480]{2,1,0:T(8,128)(2,1)} %constant.51.clone) | copy-start | bytes 2488324
  49.8 18.4 %collective-permute-start.1 = (bf16[768,512]{1,0:T(8,128)(2,1)}, bf16[768,512]{1,0:T(8,128)(2,1)S(1)}, u32[]{:S(2)}, u32[]{:S(2)}) collective-permute-start(bf16[768,512]{1,0:T(8,128)(2,1)} %get-tuple-element.14), channel_id=1, source_target_pairs={{0,4},{4,8},{8,12},{12,16},{16,20},{20,24},{24,28},{28,32},{32,36}... | collective-permute-start | bytes 2359304 | tf_op jit(solution)/shard_map/ppermute | solution.py:197
  54.0 10.1 %collective-permute-start.3 = (bf16[48,512]{1,0:T(8,128)(2,1)S(1)}, bf16[48,512]{1,0:T(8,128)(2,1)S(1)}, u32[]{:S(2)}, u32[]{:S(2)}) collective-permute-start(bf16[48,512]{1,0:T(8,128)(2,1)S(1)} %slice.21), channel_id=1, source_target_pairs={{0,228},{4,232},{8,236},{12,240},{16,244},{20,248},{24,252},{28,19... | collective-permute-start | bytes 147464 | tf_op jit(solution)/shard_map/ppermute | solution.py:199
  59.7 8.5 %collective-permute-start.2 = (bf16[64,512]{1,0:T(8,128)(2,1)S(1)}, bf16[64,512]{1,0:T(8,128)(2,1)S(1)}, u32[]{:S(2)}, u32[]{:S(2)}) collective-permute-start(bf16[64,512]{1,0:T(8,128)(2,1)S(1)} %slice.20), channel_id=1, source_target_pairs={{0,224},{4,228},{8,232},{12,236},{16,240},{20,244},{24,248},{28,25... | collective-permute-start | bytes 196616 | tf_op jit(solution)/shard_map/ppermute | solution.py:198
  73.0 13.8 %collective-permute-start.5 = (bf16[2,32,16,128]{3,2,1,0:T(8,128)(2,1)S(1)}, bf16[2,32,16,128]{3,2,1,0:T(8,128)(2,1)S(1)}, u32[]{:S(2)}, u32[]{:S(2)}) collective-permute-start(bf16[2,32,16,128]{3,2,1,0:T(8,128)(2,1)S(1)} %get-tuple-element.19), channel_id=1, source_target_pairs={{0,2},{4,6},{8,10},{12,14},{16,18},{20,22},{24,26},{28,30},{32,34}... | collective-permute-start | bytes 786440 | tf_op jit(solution)/shard_map/ppermute | solution.py:213
  76.5 14.0 %collective-permute-start.4 = (bf16[2,32,16,128]{3,2,1,0:T(8,128)(2,1)S(1)}, bf16[2,32,16,128]{3,2,1,0:T(8,128)(2,1)S(1)}, u32[]{:S(2)}, u32[]{:S(2)}) collective-permute-start(bf16[2,32,16,128]{3,2,1,0:T(8,128)(2,1)S(1)} %get-tuple-element.20), channel_id=1, source_target_pairs={{0,0},{4,4},{8,8},{12,12},{16,16},{20,20},{24,24},{28,28},{32,32},... | collective-permute-start | bytes 786440 | tf_op jit(solution)/shard_map/ppermute | solution.py:213
  90.5 11.4 %collective-permute-start.6 = (bf16[2,32,16,128]{3,2,1,0:T(8,128)(2,1)S(1)}, bf16[2,32,16,128]{3,2,1,0:T(8,128)(2,1)S(1)}, u32[]{:S(2)}, u32[]{:S(2)}) collective-permute-start(bf16[2,32,16,128]{3,2,1,0:T(8,128)(2,1)S(1)} %pad_maximum_fusion.1), channel_id=1, source_target_pairs={{0,1},{1,0},{2,3},{3,2},{4,5},{5,4},{6,7},{7,6},{8,9},{9,8},{10,11... | collective-permute-start | bytes 786440 | tf_op jit(solution)/shard_map/ppermute | solution.py:215

commit v4 on v3

--- a/solution.py
+++ b/solution.py
@@ -77,13 +77,16 @@
         out_ref[k ^ flips, 0] = rows[8 * k : 8 * k + 8].astype(BF)
 
 
-def mask_rows(region_ref, rows_ref, masked_ref, halo_ref):
+def mask_rows(region_ref, rows_ref, masked_ref, halo_ref, tail_ref, corner_ref):
     upper = one_hot(48, 64, lambda row, source: source == row + 2 * ((row * 43) >> 8) + 2)
     for pair in range(16):
         keep = region_ref[0, pair].astype(F32).astype(BF)
         rows = rows_ref[64 * pair : 64 * pair + 64, :] * keep
         masked_ref[64 * pair : 64 * pair + 64, :] = rows
-        halo_ref[48 * pair : 48 * pair + 48, :] = dot(upper, rows).astype(BF)
+        upper_rows = dot(upper, rows).astype(BF)
+        halo_ref[48 * pair : 48 * pair + 48, :] = upper_rows
+    tail_ref[...] = rows
+    corner_ref[...] = upper_rows
 
 
 def operand(first, parts):
@@ -187,16 +190,16 @@
     second = jnp.concatenate([straight, earlier], 0)
 
     rows, own_kernel, halo_kernel, bias, second = lax.optimization_barrier((rows, own_kernel, halo_kernel, bias, second))
-    own, upper_rows = pl.pallas_call(
+    own, upper_rows, tail, corner = pl.pallas_call(
         mask_rows,
         in_specs=[SMEM, VMEM],
-        out_specs=[VMEM, VMEM],
-        out_shape=[jax.ShapeDtypeStruct((1024, 512), BF), jax.ShapeDtypeStruct((768, 512), BF)],
+        out_specs=[VMEM] * 4,
+        out_shape=[jax.ShapeDtypeStruct((n, 512), BF) for n in (1024, 768, 64, 48)],
         compiler_params=PARAMS,
     )(keep, rows.reshape(1024, 512))
     zed = lax.ppermute(upper_rows, FINE, Z_ROUTE)
-    why = lax.ppermute(own[960:1024], FINE, Y_ROUTE)
-    both = lax.ppermute(upper_rows[720:768], FINE, ZY_ROUTE)
+    why = lax.ppermute(tail, FINE, Y_ROUTE)
+    both = lax.ppermute(corner, FINE, ZY_ROUTE)
     pieces = pl.pallas_call(
         encode,
         in_specs=[SMEM] + [VMEM] * 8,

time: 103 us -> 103 us (level)
  transfers between devices with their start and end apart: 8 -> 8, of which waited for: 6 -> 6; matrix products, arithmetic and copies ran while one was open for 3% -> 2% of each run, Pallas kernels for 0% -> 0%
where the time goes in v4:
time: 103 us
  starting transfers between devices  50 us (49%)
  waiting for transfers between devices  37.8 us (37%)
  Pallas kernels  11.6 us (11%)
  matrix products  1.85 us (2%)
  local copies, waits for them, and re-layouts  1.26 us (1%)
    all_to_all x1, waiting for transfers between devices, body(): lax.all_to_all(split.reshape(128, 8, 512), REGION, split_axis=0, concat_a...  21.4 us
    all_to_all x1, starting transfers between devices, body(): lax.all_to_all(split.reshape(128, 8, 512), REGION, split_axis=0, concat_a...  14.7 us
    ppermute x1, starting transfers between devices, body(): other = lax.ppermute(away, FINE, CORE_ROUTE)  10.9 us
    ppermute x2, waiting for transfers between devices, body(): lax.ppermute(pieces[2 * i:2 * i + 2], FINE, OUT_ROUTES[i])  8.84 us
    ppermute x2, starting transfers between devices, body(): lax.ppermute(pieces[2 * i:2 * i + 2], FINE, OUT_ROUTES[i])  8.06 us
    ppermute x1, starting transfers between devices, body(): both = lax.ppermute(corner, FINE, ZY_ROUTE)  5.67 us
    pallas_call x1, Pallas kernels, body(): pl.pallas_call(encode, in_specs=[SMEM] + [VMEM] * 8, out_specs=VMEM, out_...  4.82 us
    ppermute x1, starting transfers between devices, body(): keep = lax.ppermute(region, FINE, REGION_ROUTE)  4.49 us
  transfers between devices with their start and end apart: 8, of which 6 were waited for; matrix products, arithmetic and copies ran while one was open for 2% of the time, Pallas kernels for 0%

profile of v4, /device:TPU:321, one launch (start us, length us, event | category | flops | bytes accessed | tf_op | source)
XLA Modules:
  0.0 102.9 jit_solution(2404788022275133756)
XLA Ops:
  0.0 4.1 %shard_map.73 = bf16[32,4,8,512]{3,2,1,0:T(8,128)(2,1)} custom-call(bf16[512,2,512]{2,1,0:T(2,128)(2,1)} %bitcast.33), custom_call_target="tpu_custom_call" | custom-call | tf_op jit(solution)/shard_map/pallas_call | solution.py:173
  4.1 14.7 %all-to-all-start = ((bf16[128,8,512]{2,1,0:T(8,128)(2,1)}), bf16[128,8,512]{2,1,0:T(8,128)(2,1)S(1)}, u32[]{:S(2)}, u32[]{:S(2)}) async-start(bf16[128,8,512]{2,1,0:T(8,128)(2,1)} %bitcast.32), calls=%async_computation | async-start | bytes 2097152 | tf_op jit(solution)/shard_map/all_to_all | solution.py:182
  18.8 4.5 %collective-permute-start = (s32[1,16]{1,0:T(1,128)S(1)}, s32[1,16]{1,0:T(1,128)S(1)}, u32[]{:S(2)}, u32[]{:S(2)}) collective-permute-start(s32[1,16]{1,0:T(1,128)S(1)} %copy-done.4), channel_id=1, source_target_pairs={{0,0},{4,4},{8,8},{12,12},{16,16},{20,20},{24,24},{28,28},{32,32},... | collective-permute-start | bytes 200 | tf_op jit(solution)/shard_map/ppermute | solution.py:172
  23.4 0.6 copy-done.3
  24.0 0.1 broadcast_in_dim.7
  24.2 0.2 copy.16
  24.3 0.2 copy.15
  24.6 1.6 %convolution_convert_fusion = bf16[8,480,32]{1,2,0:T(8,128)(2,1)S(1)} fusion(bf16[8,108,480]{2,1,0:T(8,128)(2,1)} %constant.52.clone, bf16[108,32]{1,0:T(8,128)(2,1)S(1)} %reshape.38), kind=kOutput, calls=%fused_computation | convolution fusion | flops 26664960 | bytes 1082112 | tf_op jit(solution)/shard_map/kh,bkm->bhm/dot_general | solution.py:185
  26.1 0.3 convolution_convert_fusion.1
  26.4 21.4 %all-to-all-done = bf16[128,8,512]{2,1,0:T(8,128)(2,1)S(1)} async-done(((bf16[128,8,512]{2,1,0:T(8,128)(2,1)}), bf16[128,8,512]{2,1,0:T(8,128)(2,1)S(1)}, u32[]{:S(2)}, u32[]{:S(2)}) %all-to-all-start) | async-done | bytes 1048608 | tf_op jit(solution)/shard_map/all_to_all | solution.py:182
  48.0 1.8 %shard_map.74 = (bf16[1024,512]{1,0:T(8,128)(2,1)S(1)}, bf16[768,512]{1,0:T(8,128)(2,1)}, bf16[64,512]{1,0:T(8,128)(2,1)S(1)}, bf16[48,512]{1,0:T(8,128)(2,1)S(1)}) custom-call(s32[1,16]{1,0:T(1,128)S(1)} %collective-permute-done.region_ref, bf16[1024,512]{1,0:T(8,128)(2,1)S(1)} %bitcast.29), custom_call_target="tpu_custom_call" | custom-call | tf_op jit(solution)/shard_map/pallas_call | solution.py:193
  49.8 3.4 %collective-permute-start.1 = (bf16[768,512]{1,0:T(8,128)(2,1)}, bf16[768,512]{1,0:T(8,128)(2,1)S(1)}, u32[]{:S(2)}, u32[]{:S(2)}) collective-permute-start(bf16[768,512]{1,0:T(8,128)(2,1)} %get-tuple-element.16), channel_id=1, source_target_pairs={{0,4},{4,8},{8,12},{12,16},{16,20},{20,24},{24,28},{28,32},{32,36}... | collective-permute-start | bytes 2359304 | tf_op jit(solution)/shard_map/ppermute | solution.py:200
  53.2 5.7 %collective-permute-start.3 = (bf16[48,512]{1,0:T(8,128)(2,1)S(1)}, bf16[48,512]{1,0:T(8,128)(2,1)S(1)}, u32[]{:S(2)}, u32[]{:S(2)}) collective-permute-start(bf16[48,512]{1,0:T(8,128)(2,1)S(1)} %get-tuple-element.18), channel_id=1, source_target_pairs={{0,228},{4,232},{8,236},{12,240},{16,244},{20,248},{24,252},{28,19... | collective-permute-start | bytes 147464 | tf_op jit(solution)/shard_map/ppermute | solution.py:202
  58.9 2.8 %collective-permute-start.2 = (bf16[64,512]{1,0:T(8,128)(2,1)S(1)}, bf16[64,512]{1,0:T(8,128)(2,1)S(1)}, u32[]{:S(2)}, u32[]{:S(2)}) collective-permute-start(bf16[64,512]{1,0:T(8,128)(2,1)S(1)} %get-tuple-element.17), channel_id=1, source_target_pairs={{0,224},{4,228},{8,232},{12,236},{16,240},{20,244},{24,248},{28,25... | collective-permute-start | bytes 196616 | tf_op jit(solution)/shard_map/ppermute | solution.py:201
  61.8 2.3 %collective-permute-done.3.both_ref = bf16[48,512]{1,0:T(8,128)(2,1)S(1)} collective-permute-done((bf16[48,512]{1,0:T(8,128)(2,1)S(1)}, bf16[48,512]{1,0:T(8,128)(2,1)S(1)}, u32[]{:S(2)}, u32[]{:S(2)}) %collective-permute-start.3) | collective-permute-done | bytes 49184 | tf_op jit(solution)/shard_map/ppermute | solution.py:202
  64.1 4.1 %collective-permute-done.2.why_ref = bf16[64,512]{1,0:T(8,128)(2,1)S(1)} collective-permute-done((bf16[64,512]{1,0:T(8,128)(2,1)S(1)}, bf16[64,512]{1,0:T(8,128)(2,1)S(1)}, u32[]{:S(2)}, u32[]{:S(2)}) %collective-permute-start.2) | collective-permute-done | bytes 65568 | tf_op jit(solution)/shard_map/ppermute | solution.py:201
  68.2 4.8 %shard_map.75 = bf16[4,32,16,128]{3,2,1,0:T(8,128)(2,1)S(1)} custom-call(s32[2]{0:T(128)S(1)} %pad_add_fusion.place_ref, bf16[1024,512]{1,0:T(8,128)(2,1)S(1)} %get-tuple-element.15.own_ref, bf16[768,512]{1,0:T(8,128)(2,1)S(1)} %collective-permute-done.1.zed_ref, bf16[64,512]{1,0:T(8,128)(2,1)S(1)} %collective-permute-done.2.why_ref, ...), custom_call_target="tpu_custom_call" | custom-call | tf_op jit(solution)/shard_map/pallas_call | solution.py:203
  73.0 3.5 %collective-permute-start.5 = (bf16[2,32,16,128]{3,2,1,0:T(8,128)(2,1)S(1)}, bf16[2,32,16,128]{3,2,1,0:T(8,128)(2,1)S(1)}, u32[]{:S(2)}, u32[]{:S(2)}) collective-permute-start(bf16[2,32,16,128]{3,2,1,0:T(8,128)(2,1)S(1)} %get-tuple-element.23), channel_id=1, source_target_pairs={{0,2},{4,6},{8,10},{12,14},{16,18},{20,22},{24,26},{28,30},{32,34}... | collective-permute-start | bytes 786440 | tf_op jit(solution)/shard_map/ppermute | solution.py:216
  76.6 4.6 %collective-permute-start.4 = (bf16[2,32,16,128]{3,2,1,0:T(8,128)(2,1)S(1)}, bf16[2,32,16,128]{3,2,1,0:T(8,128)(2,1)S(1)}, u32[]{:S(2)}, u32[]{:S(2)}) collective-permute-start(bf16[2,32,16,128]{3,2,1,0:T(8,128)(2,1)S(1)} %get-tuple-element.24), channel_id=1, source_target_pairs={{0,0},{4,4},{8,8},{12,12},{16,16},{20,20},{24,24},{28,28},{32,32},... | collective-permute-start | bytes 786440 | tf_op jit(solution)/shard_map/ppermute | solution.py:216
  81.1 5.2 %collective-permute-done.5.b_ref = bf16[2,32,16,128]{3,2,1,0:T(8,128)(2,1)S(1)} collective-permute-done((bf16[2,32,16,128]{3,2,1,0:T(8,128)(2,1)S(1)}, bf16[2,32,16,128]{3,2,1,0:T(8,128)(2,1)S(1)}, u32[]{:S(2)}, u32[]{:S(2)}) %collective-permute-start.5) | collective-permute-done | bytes 262176 | tf_op jit(solution)/shard_map/ppermute | solution.py:216
  86.4 3.6 %collective-permute-done.4.a_ref = bf16[2,32,16,128]{3,2,1,0:T(8,128)(2,1)S(1)} collective-permute-done((bf16[2,32,16,128]{3,2,1,0:T(8,128)(2,1)S(1)}, bf16[2,32,16,128]{3,2,1,0:T(8,128)(2,1)S(1)}, u32[]{:S(2)}, u32[]{:S(2)}) %collective-permute-start.4) | collective-permute-done | bytes 262176 | tf_op jit(solution)/shard_map/ppermute | solution.py:216
  90.0 10.9 %collective-permute-start.6 = (bf16[2,32,16,128]{3,2,1,0:T(8,128)(2,1)S(1)}, bf16[2,32,16,128]{3,2,1,0:T(8,128)(2,1)S(1)}, u32[]{:S(2)}, u32[]{:S(2)}) collective-permute-start(bf16[2,32,16,128]{3,2,1,0:T(8,128)(2,1)S(1)} %pad_maximum_fusion.1), channel_id=1, source_target_pairs={{0,1},{1,0},{2,3},{3,2},{4,5},{5,4},{6,7},{7,6},{8,9},{9,8},{10,11... | collective-permute-start | bytes 786440 | tf_op jit(solution)/shard_map/ppermute | solution.py:218
  100.9 1.1 %collective-permute-done.6.other_ref = bf16[2,32,16,128]{3,2,1,0:T(8,128)(2,1)S(1)} collective-permute-done((bf16[2,32,16,128]{3,2,1,0:T(8,128)(2,1)S(1)}, bf16[2,32,16,128]{3,2,1,0:T(8,128)(2,1)S(1)}, u32[]{:S(2)}, u32[]{:S(2)}) %collective-permute-start.6) | collective-permute-done | bytes 262176 | tf_op jit(solution)/shard_map/ppermute | solution.py:218
  102.1 0.9 shard_map.76
  (23 shorter events, 0.4 us)
Async XLA Ops:
  4.1 14.7 %copy-start.4 = (s32[1,16]{1,0:T(1,128)S(1)}, s32[1,16]{1,0:T(1,128)}, u32[]{:S(2)}) copy-start(s32[1,16]{1,0:T(1,128)} %param.8) | copy-start | bytes 196
  4.1 19.2 %copy-start.1 = (bf16[128,32,3,3,3]{0,1,4,3,2:T(8,128)(2,1)S(1)}, bf16[128,32,3,3,3]{0,1,4,3,2:T(8,128)(2,1)}, u32[]{:S(2)}) copy-start(bf16[128,32,3,3,3]{0,1,4,3,2:T(8,128)(2,1)} %param.11) | copy-start | bytes 663556
  4.1 43.8 %all-to-all-start = ((bf16[128,8,512]{2,1,0:T(8,128)(2,1)}), bf16[128,8,512]{2,1,0:T(8,128)(2,1)S(1)}, u32[]{:S(2)}, u32[]{:S(2)}) async-start(bf16[128,8,512]{2,1,0:T(8,128)(2,1)} %bitcast.32), calls=%async_computation | async-start | bytes 2097152 | tf_op jit(solution)/shard_map/all_to_all | solution.py:182
  18.8 29.1 %collective-permute-start = (s32[1,16]{1,0:T(1,128)S(1)}, s32[1,16]{1,0:T(1,128)S(1)}, u32[]{:S(2)}, u32[]{:S(2)}) collective-permute-start(s32[1,16]{1,0:T(1,128)S(1)} %copy-done.4), channel_id=1, source_target_pairs={{0,0},{4,4},{8,8},{12,12},{16,16},{20,20},{24,24},{28,28},{32,32},... | collective-permute-start | bytes 200 | tf_op jit(solution)/shard_map/ppermute | solution.py:172
  23.4 0.7 copy-start.3
  23.4 0.8 copy-start.2
  24.5 1.6 %copy-start = (bf16[8,108,480]{2,1,0:T(8,128)(2,1)S(1)}, bf16[8,108,480]{2,1,0:T(8,128)(2,1)}, u32[]{:S(2)}) copy-start(bf16[8,108,480]{2,1,0:T(8,128)(2,1)} %constant.51.clone) | copy-start | bytes 2488324
  49.8 18.4 %collective-permute-start.1 = (bf16[768,512]{1,0:T(8,128)(2,1)}, bf16[768,512]{1,0:T(8,128)(2,1)S(1)}, u32[]{:S(2)}, u32[]{:S(2)}) collective-permute-start(bf16[768,512]{1,0:T(8,128)(2,1)} %get-tuple-element.16), channel_id=1, source_target_pairs={{0,4},{4,8},{8,12},{12,16},{16,20},{20,24},{24,28},{28,32},{32,36}... | collective-permute-start | bytes 2359304 | tf_op jit(solution)/shard_map/ppermute | solution.py:200
  53.2 10.9 %collective-permute-start.3 = (bf16[48,512]{1,0:T(8,128)(2,1)S(1)}, bf16[48,512]{1,0:T(8,128)(2,1)S(1)}, u32[]{:S(2)}, u32[]{:S(2)}) collective-permute-start(bf16[48,512]{1,0:T(8,128)(2,1)S(1)} %get-tuple-element.18), channel_id=1, source_target_pairs={{0,228},{4,232},{8,236},{12,240},{16,244},{20,248},{24,252},{28,19... | collective-permute-start | bytes 147464 | tf_op jit(solution)/shard_map/ppermute | solution.py:202
  58.9 9.3 %collective-permute-start.2 = (bf16[64,512]{1,0:T(8,128)(2,1)S(1)}, bf16[64,512]{1,0:T(8,128)(2,1)S(1)}, u32[]{:S(2)}, u32[]{:S(2)}) collective-permute-start(bf16[64,512]{1,0:T(8,128)(2,1)S(1)} %get-tuple-element.17), channel_id=1, source_target_pairs={{0,224},{4,228},{8,232},{12,236},{16,240},{20,244},{24,248},{28,25... | collective-permute-start | bytes 196616 | tf_op jit(solution)/shard_map/ppermute | solution.py:201
  73.0 13.3 %collective-permute-start.5 = (bf16[2,32,16,128]{3,2,1,0:T(8,128)(2,1)S(1)}, bf16[2,32,16,128]{3,2,1,0:T(8,128)(2,1)S(1)}, u32[]{:S(2)}, u32[]{:S(2)}) collective-permute-start(bf16[2,32,16,128]{3,2,1,0:T(8,128)(2,1)S(1)} %get-tuple-element.23), channel_id=1, source_target_pairs={{0,2},{4,6},{8,10},{12,14},{16,18},{20,22},{24,26},{28,30},{32,34}... | collective-permute-start | bytes 786440 | tf_op jit(solution)/shard_map/ppermute | solution.py:216
  76.6 13.4 %collective-permute-start.4 = (bf16[2,32,16,128]{3,2,1,0:T(8,128)(2,1)S(1)}, bf16[2,32,16,128]{3,2,1,0:T(8,128)(2,1)S(1)}, u32[]{:S(2)}, u32[]{:S(2)}) collective-permute-start(bf16[2,32,16,128]{3,2,1,0:T(8,128)(2,1)S(1)} %get-tuple-element.24), channel_id=1, source_target_pairs={{0,0},{4,4},{8,8},{12,12},{16,16},{20,20},{24,24},{28,28},{32,32},... | collective-permute-start | bytes 786440 | tf_op jit(solution)/shard_map/ppermute | solution.py:216
  90.0 12.0 %collective-permute-start.6 = (bf16[2,32,16,128]{3,2,1,0:T(8,128)(2,1)S(1)}, bf16[2,32,16,128]{3,2,1,0:T(8,128)(2,1)S(1)}, u32[]{:S(2)}, u32[]{:S(2)}) collective-permute-start(bf16[2,32,16,128]{3,2,1,0:T(8,128)(2,1)S(1)} %pad_maximum_fusion.1), channel_id=1, source_target_pairs={{0,1},{1,0},{2,3},{3,2},{4,5},{5,4},{6,7},{7,6},{8,9},{9,8},{10,11... | collective-permute-start | bytes 786440 | tf_op jit(solution)/shard_map/ppermute | solution.py:218

commit v5 on v3

--- a/solution.py
+++ b/solution.py
@@ -15,13 +15,10 @@
 F32 = jnp.float32
 
 
-MIRROR_Y = True
-
-
 def encoder(block, slab):
     x_lo, z_hi, z_lo, y = slab >> 6, (slab >> 5) & 1, (slab >> 3) & 3, slab & 7
+    y ^= 7 * (z_lo & 1)
     z_lo ^= 3 * (z_hi ^ (block & 1))
-    y ^= 7 * z_hi * MIRROR_Y
     return (((block * 4 + z_lo) * 8 + y) * 2 + x_lo) * 2 + z_hi
 
 
@@ -71,10 +68,10 @@
         phases_ref[...] = one_hot(512, 512, lambda x, to: x == 4 * (to & 127) + (to >> 7))
 
     core = pl.program_id(0) & 1
-    flips = 24 * (core ^ lax.axis_index("z_hi")) + 7 * core * MIRROR_Y
+    flips = 24 * (core ^ lax.axis_index("z_hi"))
     rows = dot(field_ref[...].reshape(256, 512), phases_ref[...])
     for k in range(32):
-        out_ref[k ^ flips, 0] = rows[8 * k : 8 * k + 8].astype(BF)
+        out_ref[(k ^ (7 * ((k >> 3) & 1))) ^ flips, 0] = rows[8 * k : 8 * k + 8].astype(BF)
 
 
 def mask_rows(region_ref, rows_ref, masked_ref, halo_ref):
@@ -163,7 +160,7 @@
     inner = lax.axis_index("x_hi") * 2 + lax.axis_index("core")
     core = lax.axis_index("core")
     z_lo = lax.axis_index("z_lo") ^ (3 * (core ^ lax.axis_index("z_hi")))
-    slab = inner * 32 + z_lo * 8 + (lax.axis_index("y") ^ (7 * core * MIRROR_Y))
+    slab = inner * 32 + z_lo * 8 + (lax.axis_index("y") ^ (7 * (z_lo & 1)))
     place = jnp.stack([block, slab]).astype(jnp.int32)
 
     keep = lax.ppermute(region, FINE, REGION_ROUTE)

time: 103 us -> 107 us (1.039)
  the two profiles are of different devices: /device:TPU:321 before, /device:TPU:67 now
where the time goes in v5:
time: 107 us
  starting transfers between devices  51.4 us (48%)
  waiting for transfers between devices  39.3 us (37%)
  Pallas kernels  11.6 us (11%)
  local copies, waits for them, and re-layouts  2.09 us (2%)
  matrix products  1.85 us (2%)
    ppermute x2, waiting for transfers between devices, body(): lax.ppermute(pieces[2 * i:2 * i + 2], FINE, OUT_ROUTES[i])  16.8 us
    all_to_all x1, starting transfers between devices, body(): lax.all_to_all(split.reshape(128, 8, 512), REGION, split_axis=0, concat_a...  15.6 us
    all_to_all x1, waiting for transfers between devices, body(): lax.all_to_all(split.reshape(128, 8, 512), REGION, split_axis=0, concat_a...  13.5 us
    ppermute x1, starting transfers between devices, body(): keep = lax.ppermute(region, FINE, REGION_ROUTE)  12.5 us
    ppermute x2, starting transfers between devices, body(): lax.ppermute(pieces[2 * i:2 * i + 2], FINE, OUT_ROUTES[i])  8.08 us
    ppermute x1, starting transfers between devices, body(): both = lax.ppermute(upper_rows[720:768], FINE, ZY_ROUTE)  7.87 us
    ppermute x1, waiting for transfers between devices, body(): why = lax.ppermute(own[960:1024], FINE, Y_ROUTE)  7.36 us
    pallas_call x1, Pallas kernels, body(): pl.pallas_call(encode, in_specs=[SMEM] + [VMEM] * 8, out_specs=VMEM, out_...  4.83 us
  transfers between devices with their start and end apart: 8, of which 6 were waited for; matrix products, arithmetic and copies ran while one was open for 3% of the time, Pallas kernels for 0%

profile of v5, /device:TPU:67, one launch (start us, length us, event | category | flops | bytes accessed | tf_op | source)
XLA Modules:
  0.0 106.7 jit_solution(4943955245348513671)
XLA Ops:
  0.0 4.1 %shard_map.73 = bf16[32,4,8,512]{3,2,1,0:T(8,128)(2,1)} custom-call(bf16[512,2,512]{2,1,0:T(2,128)(2,1)} %bitcast.33), custom_call_target="tpu_custom_call" | custom-call | tf_op jit(solution)/shard_map/pallas_call | solution.py:167
  4.1 15.6 %all-to-all-start = ((bf16[128,8,512]{2,1,0:T(8,128)(2,1)}), bf16[128,8,512]{2,1,0:T(8,128)(2,1)S(1)}, u32[]{:S(2)}, u32[]{:S(2)}) async-start(bf16[128,8,512]{2,1,0:T(8,128)(2,1)} %bitcast.32), calls=%async_computation | async-start | bytes 2097152 | tf_op jit(solution)/shard_map/all_to_all | solution.py:176
  19.7 12.5 %collective-permute-start = (s32[1,16]{1,0:T(1,128)S(1)}, s32[1,16]{1,0:T(1,128)S(1)}, u32[]{:S(2)}, u32[]{:S(2)}) collective-permute-start(s32[1,16]{1,0:T(1,128)S(1)} %copy-done.4), channel_id=1, source_target_pairs={{0,0},{4,4},{8,8},{12,12},{16,16},{20,20},{24,24},{28,28},{32,60},... | collective-permute-start | bytes 200 | tf_op jit(solution)/shard_map/ppermute | solution.py:166
  32.3 0.6 copy-done.3
  33.1 0.2 copy.16
  33.2 0.2 copy.15
  33.5 1.6 %convolution_convert_fusion = bf16[8,480,32]{1,2,0:T(8,128)(2,1)S(1)} fusion(bf16[8,108,480]{2,1,0:T(8,128)(2,1)} %constant.52.clone, bf16[108,32]{1,0:T(8,128)(2,1)S(1)} %reshape.38), kind=kOutput, calls=%fused_computation | convolution fusion | flops 26664960 | bytes 1082112 | tf_op jit(solution)/shard_map/kh,bkm->bhm/dot_general | solution.py:179
  35.0 0.3 convolution_convert_fusion.1
  35.3 13.5 %all-to-all-done = bf16[128,8,512]{2,1,0:T(8,128)(2,1)S(1)} async-done(((bf16[128,8,512]{2,1,0:T(8,128)(2,1)}), bf16[128,8,512]{2,1,0:T(8,128)(2,1)S(1)}, u32[]{:S(2)}, u32[]{:S(2)}) %all-to-all-start) | async-done | bytes 1048608 | tf_op jit(solution)/shard_map/all_to_all | solution.py:176
  48.9 1.8 %shard_map.74 = (bf16[1024,512]{1,0:T(8,128)(2,1)S(1)}, bf16[768,512]{1,0:T(8,128)(2,1)}) custom-call(s32[1,16]{1,0:T(1,128)S(1)} %collective-permute-done.region_ref, bf16[1024,512]{1,0:T(8,128)(2,1)S(1)} %bitcast.29), custom_call_target="tpu_custom_call" | custom-call | tf_op jit(solution)/shard_map/pallas_call | solution.py:187
  50.7 3.5 %collective-permute-start.1 = (bf16[768,512]{1,0:T(8,128)(2,1)}, bf16[768,512]{1,0:T(8,128)(2,1)S(1)}, u32[]{:S(2)}, u32[]{:S(2)}) collective-permute-start(bf16[768,512]{1,0:T(8,128)(2,1)} %get-tuple-element.14), channel_id=1, source_target_pairs={{0,4},{4,8},{8,12},{12,16},{16,20},{20,24},{24,28},{28,60},{60,56}... | collective-permute-start | bytes 2359304 | tf_op jit(solution)/shard_map/ppermute | solution.py:194
  54.3 0.8 slice.21
  55.1 7.9 %collective-permute-start.3 = (bf16[48,512]{1,0:T(8,128)(2,1)S(1)}, bf16[48,512]{1,0:T(8,128)(2,1)S(1)}, u32[]{:S(2)}, u32[]{:S(2)}) collective-permute-start(bf16[48,512]{1,0:T(8,128)(2,1)S(1)} %slice.21), channel_id=1, source_target_pairs={{0,228},{4,232},{8,236},{12,240},{16,244},{20,248},{24,252},{28,22... | collective-permute-start | bytes 147464 | tf_op jit(solution)/shard_map/ppermute | solution.py:196
  63.0 1.9 %collective-permute-start.2 = (bf16[64,512]{1,0:T(8,128)(2,1)S(1)}, bf16[64,512]{1,0:T(8,128)(2,1)S(1)}, u32[]{:S(2)}, u32[]{:S(2)}) collective-permute-start(bf16[64,512]{1,0:T(8,128)(2,1)S(1)} %slice.20), channel_id=1, source_target_pairs={{0,224},{4,228},{8,232},{12,236},{16,240},{20,244},{24,248},{28,25... | collective-permute-start | bytes 196616 | tf_op jit(solution)/shard_map/ppermute | solution.py:195
  65.0 0.2 collective-permute-done.3.both_ref
  65.2 7.4 %collective-permute-done.2.why_ref = bf16[64,512]{1,0:T(8,128)(2,1)S(1)} collective-permute-done((bf16[64,512]{1,0:T(8,128)(2,1)S(1)}, bf16[64,512]{1,0:T(8,128)(2,1)S(1)}, u32[]{:S(2)}, u32[]{:S(2)}) %collective-permute-start.2) | collective-permute-done | bytes 65568 | tf_op jit(solution)/shard_map/ppermute | solution.py:195
  72.5 4.8 %shard_map.75 = bf16[4,32,16,128]{3,2,1,0:T(8,128)(2,1)S(1)} custom-call(s32[2]{0:T(128)S(1)} %pad_add_fusion.place_ref, bf16[1024,512]{1,0:T(8,128)(2,1)S(1)} %get-tuple-element.13.own_ref, bf16[768,512]{1,0:T(8,128)(2,1)S(1)} %collective-permute-done.1.zed_ref, bf16[64,512]{1,0:T(8,128)(2,1)S(1)} %collective-permute-done.2.why_ref, ...), custom_call_target="tpu_custom_call" | custom-call | tf_op jit(solution)/shard_map/pallas_call | solution.py:197
  77.4 3.9 %collective-permute-start.5 = (bf16[2,32,16,128]{3,2,1,0:T(8,128)(2,1)S(1)}, bf16[2,32,16,128]{3,2,1,0:T(8,128)(2,1)S(1)}, u32[]{:S(2)}, u32[]{:S(2)}) collective-permute-start(bf16[2,32,16,128]{3,2,1,0:T(8,128)(2,1)S(1)} %get-tuple-element.19), channel_id=1, source_target_pairs={{0,2},{4,6},{8,10},{12,14},{16,18},{20,22},{24,26},{28,30},{60,34}... | collective-permute-start | bytes 786440 | tf_op jit(solution)/shard_map/ppermute | solution.py:210
  81.3 4.2 %collective-permute-start.4 = (bf16[2,32,16,128]{3,2,1,0:T(8,128)(2,1)S(1)}, bf16[2,32,16,128]{3,2,1,0:T(8,128)(2,1)S(1)}, u32[]{:S(2)}, u32[]{:S(2)}) collective-permute-start(bf16[2,32,16,128]{3,2,1,0:T(8,128)(2,1)S(1)} %get-tuple-element.20), channel_id=1, source_target_pairs={{0,0},{4,4},{8,8},{12,12},{16,16},{20,20},{24,24},{28,28},{60,32},... | collective-permute-start | bytes 786440 | tf_op jit(solution)/shard_map/ppermute | solution.py:210
  85.5 16.0 %collective-permute-done.5.b_ref = bf16[2,32,16,128]{3,2,1,0:T(8,128)(2,1)S(1)} collective-permute-done((bf16[2,32,16,128]{3,2,1,0:T(8,128)(2,1)S(1)}, bf16[2,32,16,128]{3,2,1,0:T(8,128)(2,1)S(1)}, u32[]{:S(2)}, u32[]{:S(2)}) %collective-permute-start.5) | collective-permute-done | bytes 262176 | tf_op jit(solution)/shard_map/ppermute | solution.py:210
  101.5 0.8 collective-permute-done.4.a_ref
  102.4 1.9 %collective-permute-start.6 = (bf16[2,32,16,128]{3,2,1,0:T(8,128)(2,1)S(1)}, bf16[2,32,16,128]{3,2,1,0:T(8,128)(2,1)S(1)}, u32[]{:S(2)}, u32[]{:S(2)}) collective-permute-start(bf16[2,32,16,128]{3,2,1,0:T(8,128)(2,1)S(1)} %pad_maximum_fusion.1), channel_id=1, source_target_pairs={{0,1},{1,0},{2,3},{3,2},{4,5},{5,4},{6,7},{7,6},{8,9},{9,8},{10,11... | collective-permute-start | bytes 786440 | tf_op jit(solution)/shard_map/ppermute | solution.py:212
  104.3 1.5 %collective-permute-done.6.other_ref = bf16[2,32,16,128]{3,2,1,0:T(8,128)(2,1)S(1)} collective-permute-done((bf16[2,32,16,128]{3,2,1,0:T(8,128)(2,1)S(1)}, bf16[2,32,16,128]{3,2,1,0:T(8,128)(2,1)S(1)}, u32[]{:S(2)}, u32[]{:S(2)}) %collective-permute-start.6) | collective-permute-done | bytes 262176 | tf_op jit(solution)/shard_map/ppermute | solution.py:212
  105.8 0.9 shard_map.76
  (25 shorter events, 0.5 us)
Async XLA Ops:
  4.1 15.6 %copy-start.4 = (s32[1,16]{1,0:T(1,128)S(1)}, s32[1,16]{1,0:T(1,128)}, u32[]{:S(2)}) copy-start(s32[1,16]{1,0:T(1,128)} %param.8) | copy-start | bytes 196
  4.1 28.1 %copy-start.1 = (bf16[128,32,3,3,3]{0,1,4,3,2:T(8,128)(2,1)S(1)}, bf16[128,32,3,3,3]{0,1,4,3,2:T(8,128)(2,1)}, u32[]{:S(2)}) copy-start(bf16[128,32,3,3,3]{0,1,4,3,2:T(8,128)(2,1)} %param.11) | copy-start | bytes 663556
  4.1 44.7 %all-to-all-start = ((bf16[128,8,512]{2,1,0:T(8,128)(2,1)}), bf16[128,8,512]{2,1,0:T(8,128)(2,1)S(1)}, u32[]{:S(2)}, u32[]{:S(2)}) async-start(bf16[128,8,512]{2,1,0:T(8,128)(2,1)} %bitcast.32), calls=%async_computation | async-start | bytes 2097152 | tf_op jit(solution)/shard_map/all_to_all | solution.py:176
  19.7 29.1 %collective-permute-start = (s32[1,16]{1,0:T(1,128)S(1)}, s32[1,16]{1,0:T(1,128)S(1)}, u32[]{:S(2)}, u32[]{:S(2)}) collective-permute-start(s32[1,16]{1,0:T(1,128)S(1)} %copy-done.4), channel_id=1, source_target_pairs={{0,0},{4,4},{8,8},{12,12},{16,16},{20,20},{24,24},{28,28},{32,60},... | collective-permute-start | bytes 200 | tf_op jit(solution)/shard_map/ppermute | solution.py:166
  32.3 0.7 copy-start.3
  32.3 0.8 copy-start.2
  33.4 1.6 %copy-start = (bf16[8,108,480]{2,1,0:T(8,128)(2,1)S(1)}, bf16[8,108,480]{2,1,0:T(8,128)(2,1)}, u32[]{:S(2)}) copy-start(bf16[8,108,480]{2,1,0:T(8,128)(2,1)} %constant.51.clone) | copy-start | bytes 2488324
  50.7 21.8 %collective-permute-start.1 = (bf16[768,512]{1,0:T(8,128)(2,1)}, bf16[768,512]{1,0:T(8,128)(2,1)S(1)}, u32[]{:S(2)}, u32[]{:S(2)}) collective-permute-start(bf16[768,512]{1,0:T(8,128)(2,1)} %get-tuple-element.14), channel_id=1, source_target_pairs={{0,4},{4,8},{8,12},{12,16},{16,20},{20,24},{24,28},{28,60},{60,56}... | collective-permute-start | bytes 2359304 | tf_op jit(solution)/shard_map/ppermute | solution.py:194
  55.1 10.1 %collective-permute-start.3 = (bf16[48,512]{1,0:T(8,128)(2,1)S(1)}, bf16[48,512]{1,0:T(8,128)(2,1)S(1)}, u32[]{:S(2)}, u32[]{:S(2)}) collective-permute-start(bf16[48,512]{1,0:T(8,128)(2,1)S(1)} %slice.21), channel_id=1, source_target_pairs={{0,228},{4,232},{8,236},{12,240},{16,244},{20,248},{24,252},{28,22... | collective-permute-start | bytes 147464 | tf_op jit(solution)/shard_map/ppermute | solution.py:196
  63.0 9.5 %collective-permute-start.2 = (bf16[64,512]{1,0:T(8,128)(2,1)S(1)}, bf16[64,512]{1,0:T(8,128)(2,1)S(1)}, u32[]{:S(2)}, u32[]{:S(2)}) collective-permute-start(bf16[64,512]{1,0:T(8,128)(2,1)S(1)} %slice.20), channel_id=1, source_target_pairs={{0,224},{4,228},{8,232},{12,236},{16,240},{20,244},{24,248},{28,25... | collective-permute-start | bytes 196616 | tf_op jit(solution)/shard_map/ppermute | solution.py:195
  77.4 24.1 %collective-permute-start.5 = (bf16[2,32,16,128]{3,2,1,0:T(8,128)(2,1)S(1)}, bf16[2,32,16,128]{3,2,1,0:T(8,128)(2,1)S(1)}, u32[]{:S(2)}, u32[]{:S(2)}) collective-permute-start(bf16[2,32,16,128]{3,2,1,0:T(8,128)(2,1)S(1)} %get-tuple-element.19), channel_id=1, source_target_pairs={{0,2},{4,6},{8,10},{12,14},{16,18},{20,22},{24,26},{28,30},{60,34}... | collective-permute-start | bytes 786440 | tf_op jit(solution)/shard_map/ppermute | solution.py:210
  81.3 21.0 %collective-permute-start.4 = (bf16[2,32,16,128]{3,2,1,0:T(8,128)(2,1)S(1)}, bf16[2,32,16,128]{3,2,1,0:T(8,128)(2,1)S(1)}, u32[]{:S(2)}, u32[]{:S(2)}) collective-permute-start(bf16[2,32,16,128]{3,2,1,0:T(8,128)(2,1)S(1)} %get-tuple-element.20), channel_id=1, source_target_pairs={{0,0},{4,4},{8,8},{12,12},{16,16},{20,20},{24,24},{28,28},{60,32},... | collective-permute-start | bytes 786440 | tf_op jit(solution)/shard_map/ppermute | solution.py:210
  102.4 3.4 %collective-permute-start.6 = (bf16[2,32,16,128]{3,2,1,0:T(8,128)(2,1)S(1)}, bf16[2,32,16,128]{3,2,1,0:T(8,128)(2,1)S(1)}, u32[]{:S(2)}, u32[]{:S(2)}) collective-permute-start(bf16[2,32,16,128]{3,2,1,0:T(8,128)(2,1)S(1)} %pad_maximum_fusion.1), channel_id=1, source_target_pairs={{0,1},{1,0},{2,3},{3,2},{4,5},{5,4},{6,7},{7,6},{8,9},{9,8},{10,11... | collective-permute-start | bytes 786440 | tf_op jit(solution)/shard_map/ppermute | solution.py:212
